TPU v7x, 32 devices: a whole 2x2x4 slice. The times are simulated.
32 devices in a mesh: dev: 32 (over z, y, x, core).
Axes of the slice: x: 2, y: 2, z: 4, core: 2. Of those that a mesh axis runs over, the one named last changes fastest.
Arguments:
- images: bfloat16 [160, 197, 512], P('dev'), may hold values from -6 to 6
- cotangent: bfloat16 [160, 197, 512], P('dev'), may hold values from -6 to 6
- routes: int32 [31520, 2], P('dev'), may hold values from 0 to 3, as said below
- priority: int32 [32, 985], P('dev'), may hold values from 0 to 984, each once within a row
- image_count: int32 [32], P('dev'), may hold values from 1 to 5, 112 in all
- ln1_gain: bfloat16 [512], P('dev'), may hold values from 0.5 to 1.5
- ln1_bias: bfloat16 [512], P('dev'), may hold values from -4 to 4
- w_qkv: bfloat16 [786432], P('dev'), may hold values from -0.375 to 0.375
- b_qv: bfloat16 [1024], P('dev'), may hold values from -4 to 4
- w_out: bfloat16 [262144], P('dev'), may hold values from -0.75 to 0.75
- b_out: bfloat16 [512], P('dev'), may hold values from -4 to 4
- ln2_gain: bfloat16 [512], P('dev'), may hold values from 0.5 to 1.5
- ln2_bias: bfloat16 [512], P('dev'), may hold values from -1.5 to 1.5
- w_router: bfloat16 [2048], P('dev'), may hold values from -0.1875 to 0.1875
- w_in: bfloat16 [4194304], P('dev'), may hold values from -0.25 to 0.25
- b_in: bfloat16 [8192], P('dev'), may hold values from -4 to 4
- w_back: bfloat16 [4194304], P('dev'), may hold values from -0.375 to 0.375
- b_back: bfloat16 [2048], P('dev'), may hold values from -4 to 4
Outputs:
- blocks: bfloat16 [160, 197, 512], P('dev')
- grad_images: bfloat16 [160, 197, 512], P('dev')
- grad_ln1_gain: float32 [512], P('dev')
- grad_ln1_bias: float32 [512], P('dev')
- grad_w_qkv: float32 [786432], P('dev')
- grad_b_qv: float32 [1024], P('dev')
- grad_w_out: float32 [262144], P('dev')
- grad_b_out: float32 [512], P('dev')
- grad_ln2_gain: float32 [512], P('dev')
- grad_ln2_bias: float32 [512], P('dev')
- grad_w_router: float32 [2048], P('dev')
- grad_w_in: float32 [4194304], P('dev')
- grad_b_in: float32 [8192], P('dev')
- grad_w_back: float32 [4194304], P('dev')
- grad_b_back: float32 [2048], P('dev')
Inputs may be any that keep to these rules, and one draw needn't show every extreme that they name: `routes`: each token slot names two different experts, its first choice in column 0. `priority`: each row lists every token slot of a device once, index in image-major order; earlier entries claim expert slots first. `image_count`: a device's image slots from this count on hold padding, whose output and gradient rows are zero.
All inputs are finite; a program needn't handle non-finite values.
Results may differ from a plain program's by a relative error of at most 0.013.
The roundings to bfloat16 on the way count: a program that leaves them out, or rounds other values in their place, can miss the bound.
Values may be sent and summed in bfloat16 or wider, within the bound.
A program may use at most 192 MiB of HBM per device.

v0:
```python
import functools

import jax
import jax.numpy as jnp
from jax import lax
from jax.experimental import pallas as pl
from jax.experimental.pallas import tpu as pltpu
from jax.sharding import PartitionSpec as P

D = 512
HEADS = 8
HID = 2048
EXPERTS = 4
SEQ = 197
SLOTS = 5
HEAD_DIM = 64
CAP = 555
EPSILON = 1e-06

ROWS = -(-SEQ // 16) * 16
TOK = SLOTS * ROWS
CAPP = -(-CAP // 16) * 16
LANES = 128
WIDE = 2 * D + LANES
GROUP = EXPERTS * 2 * 2 * 2
BLOCK_IN = EXPERTS * D // GROUP
BLOCK_BACK = EXPERTS * HID // GROUP
SLOT_TILE = CAPP // 5
FT = 256
VMEM_LIMIT = 63 * 1024 * 1024
MESH = pl.DeviceIdType.MESH
FULL = slice(None)
F32 = jnp.float32
BF16 = jnp.bfloat16


def mm(a, b):
    return lax.dot_general(a, b, (((1,), (0,)), ((), ())), preferred_element_type=F32)


def mm_nt(a, b):
    return lax.dot_general(a, b, (((1,), (1,)), ((), ())), preferred_element_type=F32)


def mm_tn(a, b):
    return lax.dot_general(a, b, (((0,), (0,)), ((), ())), preferred_element_type=F32)


def iota(shape, dim):
    return lax.broadcasted_iota(jnp.int32, shape, dim)


def normalize(inputs):
    centre = inputs - jnp.mean(inputs, axis=-1, keepdims=True)
    inverse = lax.rsqrt(jnp.mean(centre * centre, axis=-1, keepdims=True) + EPSILON)
    return centre * inverse, inverse


def norm_back(grad_normed, scaled, inverse, gain):
    grad_scaled = grad_normed * gain
    return inverse * (
        grad_scaled
        - jnp.mean(grad_scaled, axis=-1, keepdims=True)
        - scaled * jnp.mean(grad_scaled * scaled, axis=-1, keepdims=True)
    )


def gelu_parts(pre):
    size = jnp.abs(pre)
    t = 1.0 / (1.0 + (0.3275911 * 0.7071067811865476) * size)
    bell = jnp.exp(-0.5 * (pre * pre))
    poly = t * (
        0.127414796
        + t * (-0.142248368 + t * (0.7107068705 + t * (-0.7265760135 + t * 0.5307027145)))
    )
    tail = poly * bell
    phi = jnp.where(pre >= 0, 1.0 - tail, tail)
    return pre * phi, phi + pre * (bell * 0.3989422804014327)


def split3(value):
    high = value.astype(BF16).astype(F32)
    rest = value - high
    mid = rest.astype(BF16).astype(F32)
    return high, mid, rest - mid


def image_rows(i):
    return pl.ds(i * ROWS if isinstance(i, int) else pl.multiple_of(i * ROWS, 16), ROWS)


def attention_forward(i, r):
    rows = image_rows(i)
    r.xs[0:SEQ, :] = r.image_at[i % 2].astype(F32)
    hidden = r.xs[...]
    scaled, _ = normalize(hidden)
    normed = (scaled * r.vec[0:1, :] + r.vec[1:2, :]).astype(BF16)
    projected = mm(normed, r.wqkv[...].reshape(D, 3 * D))
    r.qkv[rows, 0:D] = (projected[:, :D] + r.vec[2:3, :]).astype(BF16)
    r.qkv[rows, D : 2 * D] = projected[:, D : 2 * D].astype(BF16)
    r.qkv[rows, 2 * D :] = (projected[:, 2 * D :] + r.vec[3:4, :]).astype(BF16)
    lane = iota((ROWS, LANES), 1)
    column = iota((ROWS, ROWS), 1)
    for pair in range(HEADS // 2):
        at = pair * LANES
        queries = r.qkv[rows, at : at + LANES]
        keys = r.qkv[rows, D + at : D + at + LANES]
        values = r.qkv[rows, 2 * D + at : 2 * D + at + LANES]
        mixes = []
        for half in range(2):
            mine = (lane >= half * HEAD_DIM) & (lane < (half + 1) * HEAD_DIM)
            own = jnp.where(mine, queries, jnp.zeros_like(queries))
            scores = mm_nt(own, keys) * HEAD_DIM**-0.5
            scores = jnp.where(column < SEQ, scores, -1e30)
            expo = jnp.exp(scores - jnp.max(scores, axis=-1, keepdims=True))
            probs = (expo / jnp.sum(expo, axis=-1, keepdims=True)).astype(BF16)
            r.probs[i * HEADS + 2 * pair + half] = probs
            mixes.append(mm(probs, values))
        r.mix[rows, at : at + LANES] = jnp.where(lane < HEAD_DIM, mixes[0], mixes[1]).astype(BF16)
    residual = hidden + mm(r.mix[rows, :], r.wout[...].reshape(D, D)) + r.vec[4:5, :]
    r.residual[rows, :] = residual
    scaled2, _ = normalize(residual)
    normed2 = (scaled2 * r.vec[5:6, :] + r.vec[6:7, :]).astype(BF16)
    r.wide[rows, 0:D] = normed2
    logits = jnp.where(lane < EXPERTS, mm_nt(normed2, r.router[...]), -1e30)
    expo = jnp.exp(logits - jnp.max(logits, axis=-1, keepdims=True))
    gates = expo / jnp.sum(expo, axis=-1, keepdims=True)
    r.gates[rows, :] = gates
    high, mid, low = split3(gates)
    packed = high + pltpu.roll(mid, EXPERTS, 1) + pltpu.roll(low, 2 * EXPERTS, 1)
    r.wide[rows, 2 * D :] = packed.astype(BF16)
    live = jnp.where(i < r.count[0], 1.0, 0.0)
    r.xs[0:SEQ, :] = r.other_at[i % 2].astype(F32) * live
    r.wide[rows, D : 2 * D] = r.xs[...].astype(BF16)


def routing(r):
    limit = r.count[0] * ROWS
    places = r.prow.shape[1]
    lane = iota((ROWS, LANES), 1)

    def find(i, carry):
        rows = image_rows(i)
        place_row, wanted = carry
        seen = r.prow[...] == iota((ROWS, places), 0) + i * ROWS
        place = jnp.sum(
            jnp.where(seen, iota((ROWS, places), 1).astype(F32), 0.0), axis=1, keepdims=True
        )
        r.gates[rows, :] = jnp.broadcast_to(place, (ROWS, LANES))
        same = iota((ROWS, TOK), 0) + i * ROWS == iota((ROWS, TOK), 1)
        place_row = place_row + jnp.sum(jnp.where(same, place, 0.0), axis=0, keepdims=True)
        live = iota((ROWS, LANES), 0) + i * ROWS < limit
        hit0 = jnp.where((r.rcol[rows, 0:1] == lane) & live, 1.0, 0.0)
        hit1 = jnp.where((r.rcol[rows, 1:2] == lane) & live, 1.0, 0.0)
        r.wide[rows, 0:LANES] = hit0.astype(BF16)
        r.wide[rows, LANES : 2 * LANES] = hit1.astype(BF16)
        return place_row, wanted + jnp.sum(hit0, axis=0, keepdims=True)

    place_row, wanted = lax.fori_loop(
        0, SLOTS, find, (jnp.zeros((1, TOK), F32), jnp.zeros((1, LANES), F32))
    )
    r.total[0:LANES, 0:TOK] = jnp.zeros((LANES, TOK), F32)

    def count(i, carry):
        rows = image_rows(i)
        earlier = jnp.where(place_row < r.gates[rows, 0:1], 1.0, 0.0).astype(BF16)
        before = mm(earlier, r.wide[:, 0 : 2 * LANES])
        hit0, hit1 = r.wide[rows, 0:LANES] > 0, r.wide[rows, LANES : 2 * LANES] > 0
        position = jnp.where(
            hit0, before[:, 0:LANES], jnp.where(hit1, before[:, LANES:] + wanted, 1e6)
        )
        position = jnp.where(position < CAP, position, -1.0)
        r.pos_col[rows, :] = position
        same = iota((ROWS, TOK), 0) + i * ROWS == iota((ROWS, TOK), 1)
        same = jnp.where(same, 1.0, 0.0).astype(BF16)
        high = position.astype(BF16)
        low = (position - high.astype(F32)).astype(BF16)
        r.total[0:LANES, 0:TOK] += mm_tn(high, same) + mm_tn(low, same)
        return carry

    lax.fori_loop(0, SLOTS, count, 0)
    r.pos_row[...] = r.total[0:8, 0:TOK]
    r.total[0:LANES, 0:TOK] = jnp.zeros((LANES, TOK), F32)


def nothing(step):
    pass


def dispatch(e, r, beside=nothing):
    wanted = r.pos_row[pl.ds(e, 1), :]
    lane = iota((SLOT_TILE, LANES), 1)

    def tile(m, carry):
        beside(m)
        rows = pl.ds(pl.multiple_of(m * SLOT_TILE, 16), SLOT_TILE)
        slot = (iota((SLOT_TILE, TOK), 0) + m * SLOT_TILE).astype(F32)
        chosen = jnp.where(slot == wanted, 1.0, 0.0).astype(BF16)
        got = mm(chosen, r.wide[...])
        r.disp[rows, :] = got[:, 0:D].astype(BF16)
        r.up[rows, :] = got[:, D : 2 * D].astype(BF16)
        mine = (lane == e) | (lane == e + EXPERTS) | (lane == e + 2 * EXPERTS)
        gate = jnp.sum(jnp.where(mine, got[:, 2 * D :], 0.0), axis=1, keepdims=True)
        r.gate_slot[rows, :] = jnp.broadcast_to(gate, (SLOT_TILE, LANES))
        r.gexp[rows, :] = (gate * got[:, D : 2 * D]).astype(BF16)
        return carry

    lax.fori_loop(0, CAPP // SLOT_TILE, tile, 0)
    r.eo[...] = jnp.zeros_like(r.eo)
    r.gdisp[...] = jnp.zeros_like(r.gdisp)


def expert_step(e, f, k, r):
    cols = pl.ds(pl.multiple_of(f * FT, FT), FT)
    block = (k, f // 4, f // 2 % 2, f % 2)
    w_in = r.win[k, :, :, :, :, cols].reshape(D, FT)
    w_back = r.wback[block]
    disp = r.disp[...]
    gexp = r.gexp[...]
    bias = r.vec[pl.ds(16 + 4 * e + f // 2, 1), pl.ds(pl.multiple_of(f % 2 * FT, FT), FT)]
    pre = mm(disp, w_in) + bias
    grad_active = mm_nt(gexp, w_back)
    active, slope = gelu_parts(pre)
    active = active.astype(BF16)
    grad_inner = (grad_active * slope).astype(BF16)
    r.eo[...] += mm(active, w_back)
    r.gdisp[...] += mm_nt(grad_inner, w_in)
    r.wback[block] = mm_tn(active, gexp).astype(BF16)
    grad_in = mm_tn(disp, grad_inner).astype(BF16)
    r.win[k, :, :, :, :, cols] = grad_in.reshape(2, 2, 2, BLOCK_IN, FT)
    r.gvec[pl.ds(16 + 4 * e + f // 2, 1), pl.ds(pl.multiple_of(f % 2 * FT, FT), FT)] = jnp.sum(
        grad_inner.astype(F32), axis=0, keepdims=True
    )


def combine(e, r, beside=nothing):
    r.gvec[pl.ds(12 + e, 1), :] = jnp.sum(r.gexp[...].astype(F32), axis=0, keepdims=True)
    out = r.eo[...] + r.vec[pl.ds(12 + e, 1), :]
    gate = r.gate_slot[:, 0:1]
    r.disp[...] = (gate * out).astype(BF16)
    r.gexp[...] = r.gdisp[...].astype(BF16)
    high, mid, low = split3(jnp.sum(r.up[...].astype(F32) * out, axis=1, keepdims=True))
    lane = iota((CAPP, LANES), 1)
    parts = jnp.where(
        lane == e,
        high,
        jnp.where(lane == e + EXPERTS, mid, jnp.where(lane == e + 2 * EXPERTS, low, 0.0)),
    )
    r.pairs[...] = parts.astype(BF16)

    def image(i, carry):
        beside(i)
        rows = image_rows(i)
        mine = iota((ROWS, LANES), 1) == e
        wanted = jnp.sum(jnp.where(mine, r.pos_col[rows, :], 0.0), axis=1, keepdims=True)
        chosen = jnp.where(wanted == iota((ROWS, CAPP), 1).astype(F32), 1.0, 0.0).astype(BF16)
        r.total[rows, 0:D] += mm(chosen, r.disp[...])
        r.total[rows, D : 2 * D] += mm(chosen, r.gexp[...])
        r.total[rows, 2 * D :] += mm(chosen, r.pairs[...])
        return carry

    lax.fori_loop(0, SLOTS, image, 0)


def norm_backward(i, r):
    rows = image_rows(i)
    lane = iota((ROWS, LANES), 1)
    live = jnp.where(i < r.count[0], 1.0, 0.0)
    residual = r.residual[rows, :]
    r.other_at[i % 2] = ((residual + r.total[rows, 0:D]) * live)[0:SEQ, :].astype(BF16)
    pairs = r.total[rows, 2 * D :]
    gates = r.gates[rows, :]
    grad_gates = (
        pairs + pltpu.roll(pairs, LANES - EXPERTS, 1) + pltpu.roll(pairs, LANES - 2 * EXPERTS, 1)
    )
    grad_gates = jnp.where(lane < EXPERTS, grad_gates, 0.0)
    grad_logits = (
        gates * (grad_gates - jnp.sum(grad_gates * gates, axis=-1, keepdims=True))
    ).astype(BF16)
    r.gvec[8:12, :] += mm_tn(grad_logits, r.wide[rows, 0:D])[0:EXPERTS, :]
    grad_normed2 = r.total[rows, D : 2 * D] + mm(grad_logits, r.router[...])
    scaled2, inverse2 = normalize(residual)
    r.gvec[5:6, :] += jnp.sum(grad_normed2 * scaled2, axis=0, keepdims=True)
    r.gvec[6:7, :] += jnp.sum(grad_normed2, axis=0, keepdims=True)
    grad_residual = r.wide[rows, D : 2 * D].astype(F32) + norm_back(
        grad_normed2, scaled2, inverse2, r.vec[5:6, :]
    )
    r.residual[rows, :] = grad_residual
    grad_attended = grad_residual.astype(BF16)
    r.wide[rows, D : 2 * D] = grad_attended
    r.gvec[4:5, :] += jnp.sum(grad_attended.astype(F32), axis=0, keepdims=True)
    r.wide[rows, 0:D] = mm_nt(grad_attended, r.wout[...].reshape(D, D)).astype(BF16)


def attention_backward(i, r):
    rows = image_rows(i)
    lane = iota((ROWS, LANES), 1)
    for pair in range(HEADS // 2):
        at = pair * LANES
        queries = r.qkv[rows, at : at + LANES]
        keys = r.qkv[rows, D + at : D + at + LANES]
        values = r.qkv[rows, 2 * D + at : 2 * D + at + LANES]
        from_mix = r.wide[rows, at : at + LANES]
        grad_q, grad_k, grad_v = [], 0.0, 0.0
        for half in range(2):
            mine = (lane >= half * HEAD_DIM) & (lane < (half + 1) * HEAD_DIM)
            own_q = jnp.where(mine, queries, jnp.zeros_like(queries))
            own_g = jnp.where(mine, from_mix, jnp.zeros_like(from_mix))
            probs_low = r.probs[i * HEADS + 2 * pair + half]
            probs = probs_low.astype(F32)
            grad_probs = mm_nt(own_g, values)
            weighted = grad_probs * probs
            grad_scores = (
                weighted - probs * jnp.sum(weighted, axis=-1, keepdims=True)
            ).astype(BF16)
            grad_v = grad_v + mm_tn(probs_low, own_g)
            grad_k = grad_k + mm_tn(grad_scores, own_q)
            grad_q.append(mm(grad_scores, keys))
        scale = HEAD_DIM**-0.5
        joined = jnp.where(lane < HEAD_DIM, grad_q[0], grad_q[1])
        r.qkv[rows, at : at + LANES] = (joined * scale).astype(BF16)
        r.qkv[rows, D + at : D + at + LANES] = (grad_k * scale).astype(BF16)
        r.qkv[rows, 2 * D + at : 2 * D + at + LANES] = grad_v.astype(BF16)
    grads = r.qkv[rows, :]
    r.gvec[2:3, :] += jnp.sum(grads[:, 0:D].astype(F32), axis=0, keepdims=True)
    r.gvec[3:4, :] += jnp.sum(grads[:, 2 * D :].astype(F32), axis=0, keepdims=True)
    grad_normed1 = mm_nt(grads, r.wqkv[...].reshape(D, 3 * D))
    r.xs[0:SEQ, :] = r.image_at[i % 2].astype(F32)
    scaled1, inverse1 = normalize(r.xs[...])
    r.wide[rows, 0:D] = (scaled1 * r.vec[0:1, :] + r.vec[1:2, :]).astype(BF16)
    r.gvec[0:1, :] += jnp.sum(grad_normed1 * scaled1, axis=0, keepdims=True)
    r.gvec[1:2, :] += jnp.sum(grad_normed1, axis=0, keepdims=True)
    grad_in = r.residual[rows, :] + norm_back(grad_normed1, scaled1, inverse1, r.vec[0:1, :])
    r.grad_at[i % 2] = grad_in[0:SEQ, :].astype(BF16)


def wout_grad(r):
    r.wout[...] = mm_tn(r.mix[...], r.wide[:, D : 2 * D]).astype(BF16).reshape(r.wout.shape)


def wqkv_grad(half, r):
    def columns(c, carry):
        cols = pl.ds(pl.multiple_of(c * FT, FT), FT)
        grad = mm_tn(r.wide[:, 0:D], r.qkv[:, cols]).astype(BF16)
        r.wqkv[:, :, :, :, :, cols] = grad.reshape(r.wqkv.shape[:5] + (FT,))
        return carry

    steps = 3 * D // FT // 2
    lax.fori_loop(half * steps, half * steps + steps, columns, 0)


def spread_router(r):
    r.router[...] = jnp.zeros_like(r.router)
    first = r.vec[8:16, :]
    r.router[0:16, :] = jnp.concatenate(
        [jnp.where(iota((8, D), 0) < EXPERTS, first, 0.0), jnp.zeros((8, D), F32)], axis=0
    ).astype(BF16)


def pattern(shape, match):
    return jnp.where(match(iota(shape, 0), iota(shape, 1)), 1.0, 0.0).astype(BF16)


def all_vectors(r):
    packs = r.small[...].reshape(GROUP * 8, LANES).astype(BF16)
    line, column = iota((GROUP * 8, D), 0), iota((GROUP * 8, D), 1)

    def row(match, line_of):
        spread = mm(packs, pattern((LANES, D), match))
        return lambda: jnp.sum(jnp.where(line == line_of, spread, 0.0), axis=0, keepdims=True)

    sixteenth = 8 * (column >> 4)
    for index, start in ((0, 0), (1, 16), (4, 64), (5, 80), (6, 96)):
        r.vec[index : index + 1, :] = row(lambda j, c: j == start + (c & 15), sixteenth)()
    for index in range(2):
        r.vec[2 + index : 3 + index, :] = row(
            lambda j, c: j == 32 + (c & 31), 8 * (16 * index + (column >> 5))
        )()
    r.vec[7:8, :] = jnp.zeros((1, D), F32)
    for e in range(EXPERTS):
        r.vec[8 + e : 9 + e, :] = row(lambda j, c: j == 4 * (c & 15) + e, sixteenth + 1)()
        r.vec[12 + e : 13 + e, :] = row(
            lambda j, c: j == 64 + (c & 63), 8 * (8 * e + (column >> 6)) + 1
        )()
    for device in range(GROUP):
        at = (device // 8, device // 4 % 2, device // 2 % 2, device % 2)
        for line_of in range(2):
            start = device % 2 * 256 + line_of * LANES
            r.vec[16 + device // 2 : 17 + device // 2, start : start + LANES] = r.small[
                at + (slice(2 + line_of, 3 + line_of), FULL)
            ]


def own_vectors(me, r):
    row, column = iota((8, D), 0), iota((8, D), 1)
    lane, line = iota((8, LANES), 1), iota((8, LANES), 0)

    def fold(values, match):
        parts = [v.astype(BF16) for v in split3(values)]
        chosen = pattern((D, LANES), match)
        return sum(mm(v, chosen) for v in parts)

    owner = jnp.where(
        row == 2, column >> 5, jnp.where(row == 3, 16 + (column >> 5), column >> 4)
    )
    top = jnp.where(owner == me, r.gvec[0:8, :], 0.0)
    by16 = fold(top, lambda c, j: (c & 15) == j)
    by32 = fold(top, lambda c, j: (c & 31) == j)
    for name, index in dict(ln1_gain=0, ln1_bias=1, b_out=4, ln2_gain=5, ln2_bias=6).items():
        getattr(r, "out_" + name)[...] = by16[index : index + 1, 0:16]
    r.out_b_qv[...] = by32[2:3, 0:32] + by32[3:4, 0:32]
    owner = jnp.where(row < 4, column >> 4, 8 * (row - 4) + (column >> 6))
    low = jnp.where(owner == me, r.gvec[8:16, :], 0.0)
    router = jnp.where((lane & 3) == line, fold(low, lambda c, j: (c & 15) == (j >> 2)), 0.0)
    r.out_w_router[...] = jnp.sum(jnp.where(line < 4, router, 0.0), axis=0, keepdims=True)[:, 0:64]
    back = jnp.where(line < 4, 0.0, fold(low, lambda c, j: (c & 63) == j))
    r.out_b_back[...] = jnp.sum(back, axis=0, keepdims=True)[:, 0:64]
    row, column = iota((16, D), 0), iota((16, D), 1)
    bias = jnp.where(2 * row + (column >> 8) == me, r.gvec[16:32, :], 0.0)
    bias = jnp.sum(bias, axis=0, keepdims=True)
    r.out_b_in[...] = bias[:, 0:256] + bias[:, 256:512]


class Place:
    def __init__(self):
        me = lax.axis_index("dev")
        self.me, self.c, self.x, self.y, self.z = me, me % 2, me // 2 % 2, me // 4 % 2, me // 8
        self.core = self.device(self.z, self.y, self.x, 1 - self.c)
        self.over_y = self.device(self.z, 1 - self.y, self.x, self.c)
        self.over_x = self.device(self.z, self.y, 1 - self.x, self.c)

    def device(self, z, y, x, c):
        return ((z * 2 + y) * 2 + x) * 2 + c

    def plane(self, k):
        return lax.rem(self.z + k + EXPERTS, EXPERTS)

    def above(self, k):
        return self.device(self.plane(k), self.y, self.x, self.c)

    def greet(self):
        barrier = pltpu.get_barrier_semaphore()
        friends = [self.above(k) for k in range(1, EXPERTS)]
        friends += [self.core, self.over_y, self.over_x]
        for friend in friends:
            pl.semaphore_signal(barrier, inc=1, device_id=(friend,), device_id_type=MESH)
        pl.semaphore_wait(barrier, len(friends))

    def first(self, route):
        return self.over_y if route == 0 else self.over_x

    def second(self, route):
        return self.over_x if route == 0 else self.over_y


class Copies:
    def __init__(self, sems, index):
        self.sems, self.index = sems, index

    def make(self, slot, source, target, device):
        send_sem, recv_sem = self.sems
        return pltpu.make_async_remote_copy(
            src_ref=source, dst_ref=target, send_sem=send_sem.at[self.index, slot],
            recv_sem=recv_sem.at[self.index, slot], device_id=(device,), device_id_type=MESH,
        )


class SumAll(Copies):
    def __init__(self, sems, index, values, landing, place):
        super().__init__(sems, index)
        self.values, self.landing, self.p = values, landing, place

    def stage(self, step):
        p = self.p
        targets = [
            [(k, p.above(k)) for k in range(1, EXPERTS)], [(4, p.over_y)], [(5, p.over_x)],
            [(6, p.core)],
        ][step]
        return [self.make(s, self.values, self.landing.at[s - 1], d) for s, d in targets]

    def begin(self, step):
        for copy in self.stage(step):
            copy.start()

    def end(self, step):
        for copy in self.stage(step):
            copy.wait()
        if step == 0:
            self.values[...] += self.landing[0] + self.landing[1] + self.landing[2]
        else:
            self.values[...] += self.landing[2 + step]


class Gather(Copies):
    def __init__(self, sems, index, shard, full, tail, route, k, place):
        super().__init__(sems, index)
        self.shard, self.full, self.tail, self.route, self.p = shard, full, tail, route, place
        self.k = k

    def at(self, lead, y, x, c):
        return self.full.at[(lead, y, x, c) + self.tail]

    def own(self):
        return self.shard.at[self.tail] if self.tail else self.shard

    def local(self, sem):
        p = self.p
        lead = p.z if self.k is None else 0
        return pltpu.make_async_copy(self.own(), self.at(lead, p.y, p.x, p.c), sem)

    def along_z(self, arriving):
        p = self.p
        if self.k is None:
            return [
                self.make(k, self.own(), self.at(p.plane(-k) if arriving else p.z, p.y, p.x, p.c),
                          p.above(k))
                for k in range(1, EXPERTS)
            ]
        if self.k == 0:
            return []
        return [self.make(1, self.own(), self.at(self.k, p.y, p.x, p.c), p.above(-self.k))]

    def lead(self):
        return FULL if self.k is None else self.k

    def across(self, step, arriving):
        p = self.p
        y, x = p.y, p.x
        if step == 0:
            if arriving:
                y, x = (1 - y, x) if self.route == 0 else (y, 1 - x)
            device = p.first(self.route)
        else:
            if arriving:
                y, x = 1 - y, 1 - x
            y, x = (FULL, x) if self.route == 0 else (y, FULL)
            device = p.second(self.route)
        block = self.at(self.lead(), y, x, p.c)
        return self.make(4 + step, block, block, device)

    def to_core(self, step, arriving):
        p = self.p
        y, x = p.y, p.x
        if step == 1:
            y, x = (1 - y, x) if self.route == 0 else (y, 1 - x)
        elif step == 2:
            y, x = (FULL, 1 - x) if self.route == 0 else (1 - y, FULL)
        block = self.at(self.lead(), y, x, 1 - p.c if arriving else p.c)
        return self.make(6 + step, block, block, p.core)

    def start_z(self):
        for copy in self.along_z(False):
            copy.start()

    def stage(self, step):
        if step == 0:
            for copy in self.along_z(True):
                copy.wait_recv()
        else:
            self.across(step - 1, True).wait_recv()
        if step < 2:
            self.across(step, False).start()
        self.to_core(step, False).start()

    def finish(self):
        for step in range(3):
            self.to_core(step, True).wait_recv()
        for copy in self.along_z(False):
            copy.wait_send()
        for step in range(2):
            self.across(step, False).wait_send()
        for step in range(3):
            self.to_core(step, False).wait_send()


class Scatter(Copies):
    def __init__(self, sems, index, full, landing, out, tail, route, k, place):
        super().__init__(sems, index)
        self.full, self.out, self.tail, self.route, self.p, self.k = (
            full, out, tail, route, place, k,
        )
        self.from_core, self.from_first, self.from_second, self.from_z = landing

    def lead(self):
        return FULL if self.k is None else self.k

    def landed(self, ref, spare):
        if self.k is None:
            return (FULL,) * (1 + spare) + self.tail
        return (self.k % ref.shape[0],) + (FULL,) * spare + self.tail

    def to_core(self):
        p = self.p
        return self.make(0, self.full.at[(self.lead(), FULL, FULL, 1 - p.c) + self.tail],
                         self.from_core.at[self.landed(self.from_core, 2)], p.core)

    def to_first(self):
        p = self.p
        y, x = (FULL, 1 - p.x) if self.route == 0 else (1 - p.y, FULL)
        return self.make(1, self.full.at[(self.lead(), y, x, p.c) + self.tail],
                         self.from_first.at[self.landed(self.from_first, 1)],
                         p.second(self.route))

    def to_second(self):
        p = self.p
        y, x = (1 - p.y, p.x) if self.route == 0 else (p.y, 1 - p.x)
        return self.make(2, self.full.at[(self.lead(), y, x, p.c) + self.tail],
                         self.from_second.at[self.landed(self.from_second, 0)],
                         p.first(self.route))

    def along_z(self):
        p = self.p
        steps = range(1, EXPERTS) if self.k is None else ([self.k] if self.k else [])
        return [
            self.make(2 + k, self.full.at[(p.plane(k) if self.k is None else k, p.y, p.x, p.c) + self.tail],
                      self.from_z.at[(k - 1,) + self.tail], p.above(k))
            for k in steps
        ]

    def add(self, mine, landed):
        def layer(k, carry):
            for at, source in zip(mine(k), landed(k)):
                self.full[at + self.tail] = self.full[at + self.tail] + source
            return carry

        if self.k is None:
            lax.fori_loop(0, EXPERTS, layer, 0)
        else:
            layer(self.k, 0)

    def slot(self, ref, k):
        return k if self.k is None else k % ref.shape[0]

    def stage(self, step):
        p, tail = self.p, self.tail
        if step == 0:
            self.to_core().start()
        elif step == 1:
            self.to_core().wait_recv()
            spots = [(y, x) for y in range(2) for x in range(2)]
            ref = self.from_core
            self.add(lambda k: [(k, y, x, p.c) for y, x in spots],
                     lambda k: [ref[(self.slot(ref, k), y, x) + tail] for y, x in spots])
            self.to_first().start()
        elif step == 2:
            self.to_first().wait_recv()
            ref = self.from_first
            self.add(lambda k: [(k, o, p.x, p.c) if self.route == 0 else (k, p.y, o, p.c) for o in range(2)],
                     lambda k: [ref[(self.slot(ref, k), o) + tail] for o in range(2)])
            self.to_second().start()
        else:
            self.to_second().wait_recv()
            ref = self.from_second
            self.add(lambda k: [(k, p.y, p.x, p.c)],
                     lambda k: [ref[(self.slot(ref, k),) + tail]])
            for copy in self.along_z():
                copy.start()

    def collect(self):
        p, tail = self.p, self.tail
        total = self.full[((p.z if self.k is None else 0), p.y, p.x, p.c) + tail].astype(F32)
        for k in range(EXPERTS - 1):
            total = total + self.from_z[(k,) + tail].astype(F32)
        rows, columns = total.shape
        height, width = self.full.shape[-2:]
        first_row, first_column = tail[0].start or 0, tail[1].start or 0
        step = width // LANES
        for j in range(columns // LANES):
            line = first_row * step + first_column // LANES + j
            self.out[pl.ds(line, rows, stride=step), :] = total[:, j * LANES : (j + 1) * LANES]

    def drain(self):
        self.to_core().wait_send()
        self.to_first().wait_send()
        self.to_second().wait_send()
        for copy in self.along_z():
            copy.wait_send()


class Refs:
    def __init__(self, names, refs):
        for name, ref in zip(names, refs, strict=True):
            setattr(self, name, ref)


SCRATCH = dict(
    image_at=((2, SEQ, D), BF16),
    other_at=((2, SEQ, D), BF16),
    grad_at=((2, SEQ, D), BF16),
    xs=((ROWS, D), F32),
    router=((LANES, D), BF16),
    qkv=((TOK, 3 * D), BF16),
    probs=((SLOTS * HEADS, ROWS, ROWS), BF16),
    mix=((TOK, D), BF16),
    residual=((TOK, D), F32),
    wide=((TOK, WIDE), BF16),
    gates=((TOK, LANES), F32),
    pos_col=((TOK, LANES), F32),
    pos_row=((8, TOK), F32),
    disp=((CAPP, D), BF16),
    up=((CAPP, D), BF16),
    gexp=((CAPP, D), BF16),
    gate_slot=((CAPP, LANES), F32),
    pairs=((CAPP, LANES), BF16),
    eo=((CAPP, D), F32),
    gdisp=((CAPP, D), F32),
    total=((TOK, WIDE), F32),
    wqkv=((EXPERTS, 2, 2, 2, 16, 3 * D), BF16),
    wout=((EXPERTS, 2, 2, 2, 16, D), BF16),
    win=((EXPERTS, 2, 2, 2, BLOCK_IN, HID), BF16),
    wback=((EXPERTS, 2, 2, 2, BLOCK_BACK, D), BF16),
)
SHARDS = dict(wqkv=(16, 3 * D), wout=(16, D), win=(BLOCK_IN, HID), wback=(BLOCK_BACK, D))


def columns_of(width, h):
    return (FULL, slice(h * width // 2, (h + 1) * width // 2))


def rows_of(height, h):
    return (slice(h * height // 2, (h + 1) * height // 2), FULL)


SMALL = dict(
    ln1_gain=16, ln1_bias=16, b_qv=32, b_out=16, ln2_gain=16, ln2_bias=16, w_router=64, b_in=256,
    b_back=64,
)
FLAT_PIECES = [("wqkv", columns_of(3 * D, h), h) for h in range(2)]
FLAT_PIECES += [("wout", columns_of(D, h), h) for h in range(2)]
FLAT_PIECES += [("small", (), 0)]
EXPERT_PIECES = [("win", rows_of(BLOCK_IN, h), h) for h in range(2)]
EXPERT_PIECES += [("wback", rows_of(BLOCK_BACK, h), h) for h in range(2)]
LANDING = {}
for name in ("wqkv", "wout"):
    for part, lead in dict(core=(4, 2, 2), first=(4, 2), second=(4,), z=(3,)).items():
        LANDING[name, part] = (lead + SHARDS[name], BF16)
for name in ("win", "wback"):
    for part, lead in dict(core=(2, 2, 2), first=(4, 2), second=(4,), z=(3,)).items():
        LANDING[name, part] = (lead + SHARDS[name], BF16)
INPUTS = ["count", "images", "cotangent", "rcol", "prow"]


def whole_kernel(*refs):
    names = INPUTS + ["shard_small"] + ["shard_" + n for n in SHARDS]
    names += ["blocks", "gimages"] + ["out_" + n for n in SHARDS] + ["out_" + n for n in SMALL]
    names += list(SCRATCH) + ["vec", "gvec", "small", "land_gvec"]
    names += ["land_" + "_".join(key) for key in LANDING]
    names += ["local_sem", "vec_send", "vec_recv", "get_send", "get_recv", "put_send", "put_recv"]
    names += ["free_sem", "in_sem", "out_sem"]
    r = Refs(names, refs)
    p = Place()
    p.greet()

    def landing(name):
        return [getattr(r, f"land_{name}_{part}") for part in ("core", "first", "second", "z")]

    get_sems, put_sems = (r.get_send, r.get_recv), (r.put_send, r.put_recv)
    flat_get, flat_put = [], []
    for index, (name, tail, route) in enumerate(FLAT_PIECES):
        flat_get.append(
            Gather(get_sems, index, getattr(r, "shard_" + name), getattr(r, name), tail, route, None, p)
        )
        if name != "small":
            flat_put.append(
                Scatter(put_sems, index, getattr(r, name), landing(name), getattr(r, "out_" + name),
                        tail, route, None, p)
            )
    get, put = [], []
    for k in range(EXPERTS):
        get.append([])
        put.append([])
        for index, (name, tail, route) in enumerate(EXPERT_PIECES):
            index += len(FLAT_PIECES) + k * len(EXPERT_PIECES)
            get[k].append(
                Gather(get_sems, index, getattr(r, "shard_" + name), getattr(r, name), tail, route, k, p)
            )
            put[k].append(
                Scatter(put_sems, index, getattr(r, name), landing(name), getattr(r, "out_" + name),
                        tail, route, k, p)
            )

    def part(pieces, which):
        return pieces if which is None else pieces[2 * which : 2 * which + 2]

    def gather_stage(k, step, which=None):
        for piece in part(get[k], which):
            piece.start_z() if step < 0 else piece.stage(step)

    def scatter_stage(k, step, which=None):
        if step == 0 and k >= 2 and which != 1:
            pl.semaphore_wait(r.free_sem, 1)
        for piece in part(put[k], which):
            piece.stage(step)
        if step == 1 and k < 2 and which != 0:
            pl.semaphore_signal(r.free_sem, inc=1, device_id=(p.core,), device_id_type=MESH)

    def wout_stage(step):
        for piece in flat_put[2:4]:
            piece.stage(step)

    events = {
        ("start",): [("get", 0, 0, 1), ("get", 0, 1, 1), ("get", 2, -1, 1)],
        ("flat", 0): [("get", 1, -1, 1)],
        ("flat", 2): [("get", 2, -1, 0), ("get", 0, 0, 0), ("get", 1, -1, 0), ("get", 1, 0, 1)],
        ("flat", 3): [("get", 0, 1, 0)],
        ("forward", 0): [("get", 0, 2, 1), ("get", 1, 1, 1)],
        ("forward", 2): [("get", 1, 0, 0)],
        ("forward", 3): [("get", 0, 2, 0)],
        ("dispatch", 0, 1): [("get", 2, 0, 1)],
        ("dispatch", 0, 2): [("get", 3, -1, 0)],
        ("dispatch", 0, 3): [("get", 3, -1, 1)],
        ("dispatch", 0, 4): [("get", 1, 1, 0)],
        ("expert", 0, 1): [("get", 2, 0, 0)],
        ("expert", 0, 4): [("get", 2, 1, 1)],
        ("expert", 0, 7): [("get", 1, 2, 1)],
        ("combine", 0, 0): [("put", 0, 0, 0)],
        ("combine", 0, 1): [("get", 2, 1, 0)],
        ("combine", 0, 3): [("get", 1, 2, 0)],
        ("dispatch", 1, 2): [("get", 2, 2, 1)],
        ("dispatch", 1, 3): [("get", 3, 0, 1)],
        ("dispatch", 1, 4): [("get", 3, 0, 0)],
        ("expert", 1, 1): [("put", 0, 1, 0), ("put", 0, 0, 1)],
        ("expert", 1, 7): [("get", 3, 1, 1)],
        ("combine", 1, 0): [("get", 3, 1, 0)],
        ("combine", 1, 1): [("get", 2, 2, 0)],
        ("combine", 1, 2): [("put", 1, 0, 0)],
        ("dispatch", 2, 3): [("put", 1, 0, 1)],
        ("dispatch", 2, 4): [("put", 0, 2, 0)],
        ("expert", 2, 1): [("put", 0, 1, 1)],
        ("expert", 2, 3): [("put", 1, 1, 0)],
        ("expert", 2, 5): [("get", 3, 2, 1)],
        ("combine", 2, 0): [("put", 2, 0, 0)],
        ("combine", 2, 1): [("put", 1, 1, 1)],
        ("dispatch", 3, 1): [("get", 3, 2, 0)],
        ("dispatch", 3, 2): [("put", 2, 1, 0)],
        ("dispatch", 3, 3): [("put", 1, 2, 0)],
        ("expert", 3, 0): [("put", 2, 0, 1)],
        ("expert", 3, 2): [("put", 1, 2, 1), ("put", 0, 2, 1)],
        ("expert", 3, 5): [("put", 1, 3, 0)],
        ("expert", 3, 6): [("put", 2, 1, 1)],
        ("combine", 3, 1): [("put", 3, 0, 0)],
        ("combine", 3, 2): [("put", 1, 3, 1)],
        ("combine", 3, 4): [("put", 2, 2, 0)],
        ("norms", 0): [("put", 3, 0, 1), ("put", 2, 2, 1)],
        ("norms", 1): [("put", 3, 1, 0)],
        ("norms", 2): [("put", 2, 3, 0)],
        ("norms", 4): [("put", 3, 1, 1)],
        ("backward", 0): [("put", 2, 3, 1)],
        ("backward", 1): [("put", 0, 3, 0), ("out", 1), ("put", 3, 2, 0)],
        ("backward", 2): [("put", 0, 3, 1), ("put", 3, 2, 1)],
        ("backward", 3): [("out", 2)],
        ("backward", 4): [("put", 3, 3, 1), ("out", 3), ("put", 3, 3, 0)],
    }

    def beside(*key):
        def at(step):
            for (*found, when), todo in events.items():
                if tuple(found) == key:
                    pl.when(step == when)(functools.partial(act, todo))

        return at

    def act(todo):
        for kind, *what in todo:
            dict(get=gather_stage, put=scatter_stage, out=wout_stage)[kind](*what)

    def fetch(i, both):
        copies = [pltpu.make_async_copy(r.images.at[i], r.image_at.at[i % 2], r.in_sem.at[0, i % 2])]
        if both:
            copies.append(
                pltpu.make_async_copy(r.cotangent.at[i], r.other_at.at[i % 2], r.in_sem.at[1, i % 2])
            )
        return copies

    def emit_block(i):
        return [pltpu.make_async_copy(r.other_at.at[i % 2], r.blocks.at[i], r.out_sem.at[0, i % 2])]

    def emit_grad(i):
        return [pltpu.make_async_copy(r.grad_at.at[i % 2], r.gimages.at[i], r.out_sem.at[1, i % 2])]

    def start(copies):
        for copy in copies:
            copy.start()

    def wait(copies):
        for copy in copies:
            copy.wait()

    start(fetch(0, True))
    local = []
    for index, piece in enumerate(flat_get + get[0]):
        copy = piece.local(r.local_sem.at[index])
        copy.start()
        local.append(copy)
    for piece in flat_get:
        piece.start_z()
    for copy in local:
        copy.wait()
    act(events.get(("start",), ()))
    r.xs[...] = jnp.zeros_like(r.xs)
    r.gvec[...] = jnp.zeros_like(r.gvec)
    r.total[...] = jnp.zeros_like(r.total)
    for step in range(3):
        for piece in flat_get:
            piece.stage(step)
        if step == 0:
            routing(r)
        act(events.get(("flat", step), ()))
    for piece in flat_get:
        piece.finish()
    act(events.get(("flat", 3), ()))
    all_vectors(r)
    spread_router(r)

    def forward(i, carry):
        @pl.when(i + 1 < SLOTS)
        def _():
            start(fetch(i + 1, True))

        wait(fetch(i, True))
        attention_forward(i, r)
        beside("forward")(i)
        return carry

    lax.fori_loop(0, SLOTS, forward, 0)
    for k in range(EXPERTS):
        e = p.plane(k)
        dispatch(e, r, beside("dispatch", k))
        for piece in get[k]:
            piece.finish()

        def step(f, carry):
            beside("expert", k)(f)
            expert_step(e, f, k, r)
            return carry

        lax.fori_loop(0, HID // FT, step, 0)
        combine(e, r, beside("combine", k))
    start(fetch(0, False))

    def norms(i, carry):
        @pl.when(i >= 2)
        def _():
            wait(emit_block(i - 2))

        norm_backward(i, r)
        start(emit_block(i))
        beside("norms")(i)
        return carry

    lax.fori_loop(0, SLOTS, norms, 0)
    wout_grad(r)
    wqkv_put, wout_put = flat_put[0:2], flat_put[2:4]
    for piece in wout_put:
        piece.stage(0)

    def backward(i, carry):
        @pl.when(i + 1 < SLOTS)
        def _():
            start(fetch(i + 1, False))

        wait(fetch(i, False))

        @pl.when(i >= 2)
        def _():
            wait(emit_grad(i - 2))

        attention_backward(i, r)
        start(emit_grad(i))
        beside("backward")(i)
        return carry

    lax.fori_loop(0, SLOTS, backward, 0)
    sums = SumAll((r.vec_send, r.vec_recv), 0, r.gvec, r.land_gvec, p)
    sums.begin(0)
    wqkv_grad(0, r)
    wqkv_put[0].stage(0)
    wqkv_grad(1, r)
    wqkv_put[1].stage(0)
    for step in range(1, 4):
        sums.end(step - 1)
        sums.begin(step)
        for piece in wqkv_put:
            piece.stage(step)
    for k in range(1, EXPERTS):
        for piece in put[k]:
            for copy in piece.along_z():
                copy.wait_recv()
    for piece in put[0]:
        piece.collect()
    for piece in wout_put:
        for copy in piece.along_z():
            copy.wait_recv()
        piece.collect()
    sums.end(3)
    own_vectors(p.me, r)
    for piece in wqkv_put:
        for copy in piece.along_z():
            copy.wait_recv()
        piece.collect()
    for pieces in put + [flat_put]:
        for piece in pieces:
            piece.drain()
    for i in range(SLOTS - 2, SLOTS):
        wait(emit_block(i))
        wait(emit_grad(i))


def alone_kernel(*refs):
    names = INPUTS + ["pack"] + ["full_" + n for n in SHARDS]
    names += ["blocks", "gimages", "gvec"] + ["out_" + n for n in SHARDS]
    names += list(SCRATCH) + ["vec", "sem"]
    r = Refs(names, refs)

    def move(source, target):
        copy = pltpu.make_async_copy(source, target, r.sem)
        copy.start()
        copy.wait()

    for name in SHARDS:
        move(getattr(r, "full_" + name), getattr(r, name))
    r.vec[...] = r.pack[...]
    r.xs[...] = jnp.zeros_like(r.xs)
    r.gvec[...] = jnp.zeros_like(r.gvec)
    r.total[...] = jnp.zeros_like(r.total)
    spread_router(r)
    routing(r)

    def forward(i, carry):
        move(r.images.at[i], r.image_at.at[i % 2])
        move(r.cotangent.at[i], r.other_at.at[i % 2])
        attention_forward(i, r)
        return carry

    def expert(e, carry):
        dispatch(e, r)
        lax.fori_loop(0, HID // FT, lambda f, c: (expert_step(e, f, e, r), c)[1], 0)
        combine(e, r)
        return carry

    def norms(i, carry):
        norm_backward(i, r)
        move(r.other_at.at[i % 2], r.blocks.at[i])
        return carry

    def backward(i, carry):
        move(r.images.at[i], r.image_at.at[i % 2])
        attention_backward(i, r)
        move(r.grad_at.at[i % 2], r.gimages.at[i])
        return carry

    lax.fori_loop(0, SLOTS, forward, 0)
    lax.fori_loop(0, EXPERTS, expert, 0)
    lax.fori_loop(0, SLOTS, norms, 0)
    wout_grad(r)
    lax.fori_loop(0, SLOTS, backward, 0)
    for half in range(2):
        wqkv_grad(half, r)
    for name in SHARDS:
        move(getattr(r, name), getattr(r, "out_" + name))


def alone(inputs, pack, full):
    vmem = pl.BlockSpec(memory_space=pltpu.VMEM)
    hbm = pl.BlockSpec(memory_space=pltpu.HBM)
    smem = pl.BlockSpec(memory_space=pltpu.SMEM)
    shapes = [((SLOTS, SEQ, D), BF16), ((SLOTS, SEQ, D), BF16), ((32, D), F32)]
    shapes += [SCRATCH[name] for name in SHARDS]
    return pl.pallas_call(
        alone_kernel,
        out_shape=[jax.ShapeDtypeStruct(*s) for s in shapes],
        in_specs=[smem] + [hbm] * 2 + [vmem] * 3 + [hbm] * 4,
        out_specs=[hbm] * 2 + [vmem] + [hbm] * 4,
        scratch_shapes=[pltpu.VMEM(*s) for s in SCRATCH.values()]
        + [pltpu.VMEM((32, D), F32), pltpu.SemaphoreType.DMA],
        compiler_params=pltpu.CompilerParams(vmem_limit_bytes=VMEM_LIMIT),
    )(*inputs, pack, *full)


def whole(inputs, pack, shards):
    vmem = pl.BlockSpec(memory_space=pltpu.VMEM)
    hbm = pl.BlockSpec(memory_space=pltpu.HBM)
    smem = pl.BlockSpec(memory_space=pltpu.SMEM)
    shapes = [((SLOTS, SEQ, D), BF16), ((SLOTS, SEQ, D), BF16)]
    shapes += [((rows * columns // LANES, LANES), F32) for rows, columns in SHARDS.values()]
    shapes += [((1, size), F32) for size in SMALL.values()]
    count = len(FLAT_PIECES) + EXPERTS * len(EXPERT_PIECES)
    dma = pltpu.SemaphoreType.DMA
    return pl.pallas_call(
        whole_kernel,
        out_shape=[jax.ShapeDtypeStruct(*s) for s in shapes],
        in_specs=[smem] + [hbm] * 2 + [vmem] * 2 + [hbm] * 5,
        out_specs=[hbm] * 2 + [vmem] * (len(shapes) - 2),
        scratch_shapes=[pltpu.VMEM(*s) for s in SCRATCH.values()]
        + [pltpu.VMEM((32, D), F32)] * 2
        + [pltpu.VMEM((EXPERTS, 2, 2, 2, 8, LANES), F32), pltpu.VMEM((6, 32, D), F32)]
        + [pltpu.VMEM(*s) for s in LANDING.values()]
        + [dma((len(FLAT_PIECES) + len(EXPERT_PIECES),)), dma((1, 7)), dma((1, 7))]
        + [dma((count, 9)), dma((count, 9)), dma((count, 6)), dma((count, 6))]
        + [pltpu.SemaphoreType.REGULAR, dma((2, 2)), dma((2, 2))],
        compiler_params=pltpu.CompilerParams(
            collective_id=0, has_side_effects=True, vmem_limit_bytes=VMEM_LIMIT
        ),
        cost_estimate=pl.CostEstimate(
            flops=40 * 10**9, bytes_accessed=50 * 10**6, transcendentals=10**7
        ),
    )(*inputs, pack, *shards)


def per_device(
    images, cotangent, routes, priority, image_count,
    ln1_gain, ln1_bias, w_qkv, b_qv, w_out, b_out, ln2_gain, ln2_bias,
    w_router, w_in, b_in, w_back, b_back,
):
    route_rows = jnp.pad(
        routes.reshape(SLOTS, SEQ, 2), ((0, 0), (0, ROWS - SEQ), (0, 0)), constant_values=-1
    ).reshape(TOK, 2)
    place = priority[0]
    place = place + (place // SEQ) * (ROWS - SEQ)
    extra = -place.shape[0] % LANES
    place_row = jnp.pad(place, (0, extra), constant_values=-1)[None, :]
    inputs = (image_count, images, cotangent, route_rows, place_row)
    if lax.axis_size("dev") != GROUP:
        return with_collectives(
            inputs, ln1_gain, ln1_bias, w_qkv, b_qv, w_out, b_out, ln2_gain, ln2_bias,
            w_router, w_in, b_in, w_back, b_back,
        )
    small = [ln1_gain, ln1_bias, b_qv, b_out, ln2_gain, ln2_bias, None, w_router, b_back, b_in]
    pack, at = 0.0, 0
    for v in small:
        size = 16 if v is None else v.shape[0]
        if v is not None:
            pack = pack + jnp.pad(v.astype(F32), (at, 8 * LANES - at - size))
        at += size
    shards = [v.reshape(s) for v, s in zip((w_qkv, w_out, w_in, w_back), SHARDS.values())]
    blocks, gimages, *grads = whole(inputs, pack.reshape(8, LANES), shards)
    grads = dict(zip(["w_qkv", "w_out", "w_in", "w_back"] + list(SMALL), grads))
    order = ["ln1_gain", "ln1_bias", "w_qkv", "b_qv", "w_out", "b_out", "ln2_gain", "ln2_bias"]
    order += ["w_router", "w_in", "b_in", "w_back", "b_back"]
    return (blocks, gimages) + tuple(grads[name].reshape(-1) for name in order)


def with_collectives(
    inputs, ln1_gain, ln1_bias, w_qkv, b_qv, w_out, b_out, ln2_gain, ln2_bias,
    w_router, w_in, b_in, w_back, b_back,
):
    gather = lambda v: lax.all_gather(v, "dev", axis=0, tiled=True)
    scatter = lambda v: lax.psum_scatter(
        v.astype(F32).reshape(-1), "dev", scatter_dimension=0, tiled=True
    )
    row = lambda v: gather(v).astype(F32).reshape(-1, D)
    zero = jnp.zeros((1, D), F32)
    pack = jnp.concatenate(
        [row(ln1_gain), row(ln1_bias), row(b_qv), row(b_out), row(ln2_gain), row(ln2_bias), zero,
         gather(w_router).astype(F32).reshape(D, EXPERTS).T, row(b_back), row(b_in)]
    )
    full = [
        gather(v).reshape(SCRATCH[name][0]) for v, name in zip((w_qkv, w_out, w_in, w_back), SHARDS)
    ]
    blocks, gimages, gvec, gwqkv, gwout, gwin, gwback = alone(inputs, pack, full)
    return (
        blocks, gimages, scatter(gvec[0]), scatter(gvec[1]), scatter(gwqkv), scatter(gvec[2:4]),
        scatter(gwout), scatter(gvec[4]), scatter(gvec[5]), scatter(gvec[6]),
        scatter(gvec[8:12].T), scatter(gwin), scatter(gvec[16:32]), scatter(gwback),
        scatter(gvec[12:16]),
    )


def solution(mesh):
    split = P("dev")
    return jax.shard_map(
        per_device, mesh=mesh, in_specs=(split,) * 18, out_specs=(split,) * 15, check_vma=False
    )
```

profile of v0, /device:TPU:0, one launch (start us, length us, event | category | flops | bytes accessed | tf_op | source)
XLA Modules:
  0.0 228.3 jit_solution(11229042494320216811)
XLA Ops:
  1.3 0.7 fusion.1
  2.0 0.6 pad.72
  2.6 1.5 add_bitcast_fusion.refs_5_
  4.1 0.8 reshape.90
  4.8 1.3 reshape.94.refs_7_
  6.2 0.7 reshape.93.refs_6_
  6.9 1.8 reshape.95.refs_8_
  8.7 0.9 reshape.96.refs_9_
  9.8 0.8 pad.71.clone
  10.6 206.2 %shard_map.289 = (bf16[5,197,512]{2,1,0:T(8,128)(2,1)}, bf16[5,197,512]{2,1,0:T(8,128)(2,1)}, f32[192,128]{1,0:T(8,128)}, f32[64,128]{1,0:T(8,128)}, f32[1024,12...) custom-call(s32[1]{0:T(128)S(6)} %copy.51.refs_0_, ...), custom_call_target="tpu_custom_call" | custom-call | flops 40000000000 | bytes 50000000 | tf_op jit(solution)/shard_map/pallas_call | solution.py:1089
  216.9 2.3 %copy.52 = bf16[5,197,512]{2,1,0:T(8,128)(2,1)} copy(bf16[5,197,512]{2,1,0:T(8,128)(2,1)} %get-tuple-element.60) | data formatting | bytes 2017280
  219.2 1.0 copy.53
  220.2 0.5 copy.54
  220.8 0.5 copy.55
  221.3 0.6 copy.56
  221.9 0.5 copy.57
  222.4 0.6 copy.58
  223.1 0.5 copy.59
  224.3 0.5 copy.61
  225.0 0.5 copy.62
  225.5 0.8 copy.63
  226.4 0.6 copy.64
  226.9 0.8 copy.65
  227.8 0.5 copy.66
  (34 shorter events, 1.2 us)
Async XLA Ops:
  0.6 5.5 %copy-start.5 = (bf16[24576]{0:T(1024)(128)(2,1)S(1)}, bf16[24576]{0:T(1024)(128)(2,1)}, u32[]{:S(2)}) copy-start(bf16[24576]{0:T(1024)(128)(2,1)} %param.25) | copy-start | bytes 147460
  6.9 1.8 copy-start.3
  216.9 2.3 %copy-start = (bf16[5,197,512]{2,1,0:T(8,128)(2,1)S(1)}, bf16[5,197,512]{2,1,0:T(8,128)(2,1)}, u32[]{:S(2)}) copy-start(bf16[5,197,512]{2,1,0:T(8,128)(2,1)} %get-tuple-element.61) | copy-start | bytes 3025924
  219.2 1.0 copy-start.15
  219.2 2.1 copy-start.4
  219.2 6.3 %copy-start.2 = (f32[1024,128]{1,0:T(8,128)S(1)}, f32[1024,128]{1,0:T(8,128)}, u32[]{:S(2)}) copy-start(f32[1024,128]{1,0:T(8,128)} %get-tuple-element.41) | copy-start | bytes 1572868
  220.2 0.6 copy-start.14
  221.3 0.7 copy-start.13
  221.3 1.2 copy-start.6
  222.4 0.6 copy-start.12
  223.1 0.7 copy-start.11
  223.7 0.6 copy-start.10
  224.3 0.7 copy-start.9
  225.5 0.8 copy-start.7
  225.5 1.4 copy-start.1
  226.9 0.8 copy-start.8
where the time goes:
time: 229 us; the launch traced here: 228 us
  Pallas kernels  206 us (90%)
  local copies, waits for them, and re-layouts  18.5 us (8%)
    pallas_call x1, Pallas kernels, whole(): pl.pallas_call(whole_kernel, out_shape=[jax.ShapeDtypeStruct(*s) for s in...  206 us
    unnamed x48, local copies, waits for them, and re-layouts  11.6 us
    reshape x4, local copies, waits for them, and re-layouts, per_device(): v.reshape(s)  4.73 us

commit v1 on v0

--- a/solution.py
+++ b/solution.py
@@ -26,8 +26,9 @@
 BLOCK_IN = EXPERTS * D // GROUP
 BLOCK_BACK = EXPERTS * HID // GROUP
 SLOT_TILE = CAPP // 5
-FT = 256
-VMEM_LIMIT = 63 * 1024 * 1024
+FT = 512
+QKV_PARTS = 4
+VMEM_LIMIT = 65000 * 1024
 MESH = pl.DeviceIdType.MESH
 FULL = slice(None)
 F32 = jnp.float32
@@ -89,6 +90,12 @@
     return pl.ds(i * ROWS if isinstance(i, int) else pl.multiple_of(i * ROWS, 16), ROWS)
 
 
+def two_heads(block):
+    first = iota(block.shape, 1) < HEAD_DIM
+    zero = jnp.zeros_like(block)
+    return jnp.concatenate([jnp.where(first, block, zero), jnp.where(first, zero, block)], axis=0)
+
+
 def attention_forward(i, r):
     rows = image_rows(i)
     r.xs[0:SEQ, :] = r.image_at[i % 2].astype(F32)
@@ -100,23 +107,22 @@
     r.qkv[rows, D : 2 * D] = projected[:, D : 2 * D].astype(BF16)
     r.qkv[rows, 2 * D :] = (projected[:, 2 * D :] + r.vec[3:4, :]).astype(BF16)
     lane = iota((ROWS, LANES), 1)
-    column = iota((ROWS, ROWS), 1)
+    column = iota((2 * ROWS, ROWS), 1)
     for pair in range(HEADS // 2):
         at = pair * LANES
         queries = r.qkv[rows, at : at + LANES]
         keys = r.qkv[rows, D + at : D + at + LANES]
         values = r.qkv[rows, 2 * D + at : 2 * D + at + LANES]
-        mixes = []
-        for half in range(2):
-            mine = (lane >= half * HEAD_DIM) & (lane < (half + 1) * HEAD_DIM)
-            own = jnp.where(mine, queries, jnp.zeros_like(queries))
-            scores = mm_nt(own, keys) * HEAD_DIM**-0.5
-            scores = jnp.where(column < SEQ, scores, -1e30)
-            expo = jnp.exp(scores - jnp.max(scores, axis=-1, keepdims=True))
-            probs = (expo / jnp.sum(expo, axis=-1, keepdims=True)).astype(BF16)
-            r.probs[i * HEADS + 2 * pair + half] = probs
-            mixes.append(mm(probs, values))
-        r.mix[rows, at : at + LANES] = jnp.where(lane < HEAD_DIM, mixes[0], mixes[1]).astype(BF16)
+        both = two_heads(queries)
+        scores = mm_nt(both, keys) * HEAD_DIM**-0.5
+        scores = jnp.where(column < SEQ, scores, -1e30)
+        expo = jnp.exp(scores - jnp.max(scores, axis=-1, keepdims=True))
+        probs = (expo / jnp.sum(expo, axis=-1, keepdims=True)).astype(BF16)
+        r.probs[i * (HEADS // 2) + pair] = probs
+        mixed = mm(probs, values)
+        r.mix[rows, at : at + LANES] = jnp.where(
+            lane < HEAD_DIM, mixed[:ROWS], mixed[ROWS:]
+        ).astype(BF16)
     residual = hidden + mm(r.mix[rows, :], r.wout[...].reshape(D, D)) + r.vec[4:5, :]
     r.residual[rows, :] = residual
     scaled2, _ = normalize(residual)
@@ -136,22 +142,29 @@
 
 def routing(r):
     limit = r.count[0] * ROWS
-    places = r.prow.shape[1]
+    order = r.order[...]
+    places = order.shape[1]
+    for image in range(1, SLOTS):
+        order = order + jnp.where(r.order[...] >= image * SEQ, ROWS - SEQ, 0)
     lane = iota((ROWS, LANES), 1)
 
     def find(i, carry):
         rows = image_rows(i)
         place_row, wanted = carry
-        seen = r.prow[...] == iota((ROWS, places), 0) + i * ROWS
+        seen = order == iota((ROWS, places), 0) + i * ROWS
         place = jnp.sum(
             jnp.where(seen, iota((ROWS, places), 1).astype(F32), 0.0), axis=1, keepdims=True
         )
         r.gates[rows, :] = jnp.broadcast_to(place, (ROWS, LANES))
         same = iota((ROWS, TOK), 0) + i * ROWS == iota((ROWS, TOK), 1)
         place_row = place_row + jnp.sum(jnp.where(same, place, 0.0), axis=0, keepdims=True)
-        live = iota((ROWS, LANES), 0) + i * ROWS < limit
-        hit0 = jnp.where((r.rcol[rows, 0:1] == lane) & live, 1.0, 0.0)
-        hit1 = jnp.where((r.rcol[rows, 1:2] == lane) & live, 1.0, 0.0)
+        row = iota((ROWS, LANES), 0)
+        live = (row + i * ROWS < limit) & (row < SEQ)
+        own = iota((ROWS, places), 0) + i * SEQ == iota((ROWS, places), 1)
+        first = jnp.sum(jnp.where(own, r.routes[0:1, :], 0), axis=1, keepdims=True)
+        second = jnp.sum(jnp.where(own, r.routes[1:2, :], 0), axis=1, keepdims=True)
+        hit0 = jnp.where((first == lane) & live, 1.0, 0.0)
+        hit1 = jnp.where((second == lane) & live, 1.0, 0.0)
         r.wide[rows, 0:LANES] = hit0.astype(BF16)
         r.wide[rows, LANES : 2 * LANES] = hit1.astype(BF16)
         return place_row, wanted + jnp.sum(hit0, axis=0, keepdims=True)
@@ -212,12 +225,12 @@
 
 def expert_step(e, f, k, r):
     cols = pl.ds(pl.multiple_of(f * FT, FT), FT)
-    block = (k, f // 4, f // 2 % 2, f % 2)
+    block = (k, f // 2, f % 2)
     w_in = r.win[k, :, :, :, :, cols].reshape(D, FT)
-    w_back = r.wback[block]
+    w_back = r.wback[block].reshape(FT, D)
     disp = r.disp[...]
     gexp = r.gexp[...]
-    bias = r.vec[pl.ds(16 + 4 * e + f // 2, 1), pl.ds(pl.multiple_of(f % 2 * FT, FT), FT)]
+    bias = r.vec[pl.ds(16 + 4 * e + f, 1), :]
     pre = mm(disp, w_in) + bias
     grad_active = mm_nt(gexp, w_back)
     active, slope = gelu_parts(pre)
@@ -225,10 +238,10 @@
     grad_inner = (grad_active * slope).astype(BF16)
     r.eo[...] += mm(active, w_back)
     r.gdisp[...] += mm_nt(grad_inner, w_in)
-    r.wback[block] = mm_tn(active, gexp).astype(BF16)
+    r.wback[block] = mm_tn(active, gexp).astype(BF16).reshape(2, BLOCK_BACK, D)
     grad_in = mm_tn(disp, grad_inner).astype(BF16)
     r.win[k, :, :, :, :, cols] = grad_in.reshape(2, 2, 2, BLOCK_IN, FT)
-    r.gvec[pl.ds(16 + 4 * e + f // 2, 1), pl.ds(pl.multiple_of(f % 2 * FT, FT), FT)] = jnp.sum(
+    r.gvec[pl.ds(16 + 4 * e + f, 1), :] = jnp.sum(
         grad_inner.astype(F32), axis=0, keepdims=True
     )
 
@@ -301,25 +314,20 @@
         keys = r.qkv[rows, D + at : D + at + LANES]
         values = r.qkv[rows, 2 * D + at : 2 * D + at + LANES]
         from_mix = r.wide[rows, at : at + LANES]
-        grad_q, grad_k, grad_v = [], 0.0, 0.0
-        for half in range(2):
-            mine = (lane >= half * HEAD_DIM) & (lane < (half + 1) * HEAD_DIM)
-            own_q = jnp.where(mine, queries, jnp.zeros_like(queries))
-            own_g = jnp.where(mine, from_mix, jnp.zeros_like(from_mix))
-            probs_low = r.probs[i * HEADS + 2 * pair + half]
-            probs = probs_low.astype(F32)
-            grad_probs = mm_nt(own_g, values)
-            weighted = grad_probs * probs
-            grad_scores = (
-                weighted - probs * jnp.sum(weighted, axis=-1, keepdims=True)
-            ).astype(BF16)
-            grad_v = grad_v + mm_tn(probs_low, own_g)
-            grad_k = grad_k + mm_tn(grad_scores, own_q)
-            grad_q.append(mm(grad_scores, keys))
+        from_both = two_heads(from_mix)
+        probs_low = r.probs[i * (HEADS // 2) + pair]
+        probs = probs_low.astype(F32)
+        weighted = mm_nt(from_both, values) * probs
+        grad_scores = (
+            weighted - probs * jnp.sum(weighted, axis=-1, keepdims=True)
+        ).astype(BF16)
+        grad_q = mm(grad_scores, keys)
         scale = HEAD_DIM**-0.5
-        joined = jnp.where(lane < HEAD_DIM, grad_q[0], grad_q[1])
+        joined = jnp.where(lane < HEAD_DIM, grad_q[:ROWS], grad_q[ROWS:])
         r.qkv[rows, at : at + LANES] = (joined * scale).astype(BF16)
+        grad_k = mm_tn(grad_scores, two_heads(queries))
         r.qkv[rows, D + at : D + at + LANES] = (grad_k * scale).astype(BF16)
+        grad_v = mm_tn(probs_low, from_both)
         r.qkv[rows, 2 * D + at : 2 * D + at + LANES] = grad_v.astype(BF16)
     grads = r.qkv[rows, :]
     r.gvec[2:3, :] += jnp.sum(grads[:, 0:D].astype(F32), axis=0, keepdims=True)
@@ -338,15 +346,11 @@
     r.wout[...] = mm_tn(r.mix[...], r.wide[:, D : 2 * D]).astype(BF16).reshape(r.wout.shape)
 
 
-def wqkv_grad(half, r):
-    def columns(c, carry):
-        cols = pl.ds(pl.multiple_of(c * FT, FT), FT)
-        grad = mm_tn(r.wide[:, 0:D], r.qkv[:, cols]).astype(BF16)
-        r.wqkv[:, :, :, :, :, cols] = grad.reshape(r.wqkv.shape[:5] + (FT,))
-        return carry
-
-    steps = 3 * D // FT // 2
-    lax.fori_loop(half * steps, half * steps + steps, columns, 0)
+def wqkv_grad(part, r):
+    width = 3 * D // QKV_PARTS
+    cols = slice(part * width, (part + 1) * width)
+    grad = mm_tn(r.wide[:, 0:D], r.qkv[:, cols]).astype(BF16)
+    r.wqkv[:, :, :, :, :, cols] = grad.reshape(r.wqkv.shape[:5] + (width,))
 
 
 def spread_router(r):
@@ -690,7 +694,7 @@
     xs=((ROWS, D), F32),
     router=((LANES, D), BF16),
     qkv=((TOK, 3 * D), BF16),
-    probs=((SLOTS * HEADS, ROWS, ROWS), BF16),
+    probs=((SLOTS * HEADS // 2, 2 * ROWS, ROWS), BF16),
     mix=((TOK, D), BF16),
     residual=((TOK, D), F32),
     wide=((TOK, WIDE), BF16),
@@ -713,8 +717,8 @@
 SHARDS = dict(wqkv=(16, 3 * D), wout=(16, D), win=(BLOCK_IN, HID), wback=(BLOCK_BACK, D))
 
 
-def columns_of(width, h):
-    return (FULL, slice(h * width // 2, (h + 1) * width // 2))
+def columns_of(width, h, parts=2):
+    return (FULL, slice(h * width // parts, (h + 1) * width // parts))
 
 
 def rows_of(height, h):
@@ -725,7 +729,7 @@
     ln1_gain=16, ln1_bias=16, b_qv=32, b_out=16, ln2_gain=16, ln2_bias=16, w_router=64, b_in=256,
     b_back=64,
 )
-FLAT_PIECES = [("wqkv", columns_of(3 * D, h), h) for h in range(2)]
+FLAT_PIECES = [("wqkv", columns_of(3 * D, h, QKV_PARTS), h % 2) for h in range(QKV_PARTS)]
 FLAT_PIECES += [("wout", columns_of(D, h), h) for h in range(2)]
 FLAT_PIECES += [("small", (), 0)]
 EXPERT_PIECES = [("win", rows_of(BLOCK_IN, h), h) for h in range(2)]
@@ -737,7 +741,7 @@
 for name in ("win", "wback"):
     for part, lead in dict(core=(2, 2, 2), first=(4, 2), second=(4,), z=(3,)).items():
         LANDING[name, part] = (lead + SHARDS[name], BF16)
-INPUTS = ["count", "images", "cotangent", "rcol", "prow"]
+INPUTS = ["count", "images", "cotangent", "routes", "order"]
 
 
 def whole_kernel(*refs):
@@ -795,61 +799,61 @@
             pl.semaphore_signal(r.free_sem, inc=1, device_id=(p.core,), device_id_type=MESH)
 
     def wout_stage(step):
-        for piece in flat_put[2:4]:
+        for piece in flat_put[QKV_PARTS:]:
             piece.stage(step)
 
     events = {
-        ("start",): [("get", 0, 0, 1), ("get", 0, 1, 1), ("get", 2, -1, 1)],
-        ("flat", 0): [("get", 1, -1, 1)],
-        ("flat", 2): [("get", 2, -1, 0), ("get", 0, 0, 0), ("get", 1, -1, 0), ("get", 1, 0, 1)],
-        ("flat", 3): [("get", 0, 1, 0)],
-        ("forward", 0): [("get", 0, 2, 1), ("get", 1, 1, 1)],
+        ("start",): [("get", 0, 0, 1), ("get", 0, 1, 1)],
+        ("flat", 0): [("get", 3, -1, 0)],
+        ("flat", 1): [("get", 3, 0, 0), ("get", 1, -1, 0)],
+        ("flat", 2): [("get", 1, -1, 1), ("get", 0, 0, 0), ("get", 3, 1, 0), ("get", 0, 2, 1), ("get", 2, -1, 0)],
+        ("forward", 0): [("get", 0, 1, 0)],
         ("forward", 2): [("get", 1, 0, 0)],
-        ("forward", 3): [("get", 0, 2, 0)],
-        ("dispatch", 0, 1): [("get", 2, 0, 1)],
-        ("dispatch", 0, 2): [("get", 3, -1, 0)],
-        ("dispatch", 0, 3): [("get", 3, -1, 1)],
-        ("dispatch", 0, 4): [("get", 1, 1, 0)],
-        ("expert", 0, 1): [("get", 2, 0, 0)],
-        ("expert", 0, 4): [("get", 2, 1, 1)],
-        ("expert", 0, 7): [("get", 1, 2, 1)],
-        ("combine", 0, 0): [("put", 0, 0, 0)],
-        ("combine", 0, 1): [("get", 2, 1, 0)],
-        ("combine", 0, 3): [("get", 1, 2, 0)],
-        ("dispatch", 1, 2): [("get", 2, 2, 1)],
-        ("dispatch", 1, 3): [("get", 3, 0, 1)],
-        ("dispatch", 1, 4): [("get", 3, 0, 0)],
-        ("expert", 1, 1): [("put", 0, 1, 0), ("put", 0, 0, 1)],
-        ("expert", 1, 7): [("get", 3, 1, 1)],
-        ("combine", 1, 0): [("get", 3, 1, 0)],
-        ("combine", 1, 1): [("get", 2, 2, 0)],
-        ("combine", 1, 2): [("put", 1, 0, 0)],
-        ("dispatch", 2, 3): [("put", 1, 0, 1)],
-        ("dispatch", 2, 4): [("put", 0, 2, 0)],
-        ("expert", 2, 1): [("put", 0, 1, 1)],
-        ("expert", 2, 3): [("put", 1, 1, 0)],
-        ("expert", 2, 5): [("get", 3, 2, 1)],
-        ("combine", 2, 0): [("put", 2, 0, 0)],
-        ("combine", 2, 1): [("put", 1, 1, 1)],
-        ("dispatch", 3, 1): [("get", 3, 2, 0)],
-        ("dispatch", 3, 2): [("put", 2, 1, 0)],
-        ("dispatch", 3, 3): [("put", 1, 2, 0)],
-        ("expert", 3, 0): [("put", 2, 0, 1)],
-        ("expert", 3, 2): [("put", 1, 2, 1), ("put", 0, 2, 1)],
-        ("expert", 3, 5): [("put", 1, 3, 0)],
-        ("expert", 3, 6): [("put", 2, 1, 1)],
-        ("combine", 3, 1): [("put", 3, 0, 0)],
-        ("combine", 3, 2): [("put", 1, 3, 1)],
-        ("combine", 3, 4): [("put", 2, 2, 0)],
-        ("norms", 0): [("put", 3, 0, 1), ("put", 2, 2, 1)],
-        ("norms", 1): [("put", 3, 1, 0)],
-        ("norms", 2): [("put", 2, 3, 0)],
-        ("norms", 4): [("put", 3, 1, 1)],
+        ("forward", 4): [("get", 1, 0, 1)],
+        ("dispatch", 0, 0): [("get", 0, 2, 0)],
+        ("dispatch", 0, 2): [("get", 2, -1, 1)],
+        ("dispatch", 0, 3): [("get", 1, 1, 0)],
+        ("dispatch", 0, 4): [("get", 3, 2, 0)],
+        ("expert", 0, 3): [("get", 1, 1, 1)],
+        ("expert", 0, 7): [("get", 1, 2, 0)],
+        ("combine", 0, 2): [("get", 2, 0, 0), ("get", 1, 2, 1), ("get", 3, -1, 1)],
+        ("combine", 0, 3): [("get", 2, 0, 1)],
+        ("combine", 0, 4): [("put", 0, 0, 0)],
+        ("dispatch", 1, 4): [("get", 2, 1, 0)],
+        ("expert", 1, 3): [("put", 0, 0, 1)],
+        ("expert", 1, 5): [("get", 3, 0, 1)],
+        ("expert", 1, 6): [("get", 2, 2, 0)],
+        ("expert", 1, 7): [("get", 2, 1, 1)],
+        ("combine", 1, 0): [("put", 1, 0, 0)],
+        ("combine", 1, 3): [("get", 3, 1, 1)],
+        ("dispatch", 2, 1): [("get", 2, 2, 1), ("put", 0, 1, 0)],
+        ("dispatch", 2, 4): [("put", 1, 0, 1), ("put", 1, 1, 0)],
+        ("expert", 2, 6): [("put", 0, 1, 1)],
+        ("expert", 2, 7): [("get", 3, 2, 1)],
+        ("combine", 2, 2): [("put", 2, 0, 0)],
+        ("combine", 2, 4): [("put", 0, 2, 0)],
+        ("dispatch", 3, 0): [("put", 1, 2, 0)],
+        ("dispatch", 3, 3): [("put", 2, 0, 1)],
+        ("expert", 3, 0): [("put", 2, 1, 0)],
+        ("expert", 3, 3): [("put", 1, 3, 0)],
+        ("expert", 3, 4): [("put", 2, 1, 1)],
+        ("expert", 3, 6): [("put", 0, 3, 0)],
+        ("expert", 3, 7): [("put", 2, 2, 0)],
+        ("combine", 3, 1): [("put", 1, 1, 1)],
+        ("combine", 3, 3): [("put", 3, 0, 0)],
+        ("norms", 0): [("put", 2, 3, 0)],
+        ("norms", 1): [("put", 2, 2, 1)],
+        ("norms", 2): [("put", 3, 1, 0)],
+        ("norms", 3): [("put", 0, 2, 1)],
         ("backward", 0): [("put", 2, 3, 1)],
-        ("backward", 1): [("put", 0, 3, 0), ("out", 1), ("put", 3, 2, 0)],
-        ("backward", 2): [("put", 0, 3, 1), ("put", 3, 2, 1)],
+        ("backward", 1): [("put", 3, 0, 1), ("out", 1), ("put", 1, 2, 1)],
+        ("backward", 2): [("put", 3, 2, 0)],
         ("backward", 3): [("out", 2)],
-        ("backward", 4): [("put", 3, 3, 1), ("out", 3), ("put", 3, 3, 0)],
+        ("backward", 4): [("put", 3, 1, 1), ("put", 1, 3, 1)],
+        ("tail", 0): [("out", 3)],
+        ("tail", 2): [("put", 3, 3, 0)],
+        ("tail", 3): [("put", 3, 2, 1), ("put", 0, 3, 1)],
+        ("tail", 4): [("put", 3, 3, 1)],
     }
 
     def beside(*key):
@@ -930,7 +934,8 @@
             piece.finish()
 
         def step(f, carry):
-            beside("expert", k)(f)
+            beside("expert", k)(2 * f)
+            beside("expert", k)(2 * f + 1)
             expert_step(e, f, k, r)
             return carry
 
@@ -950,7 +955,7 @@
 
     lax.fori_loop(0, SLOTS, norms, 0)
     wout_grad(r)
-    wqkv_put, wout_put = flat_put[0:2], flat_put[2:4]
+    wqkv_put, wout_put = flat_put[:QKV_PARTS], flat_put[QKV_PARTS:]
     for piece in wout_put:
         piece.stage(0)
 
@@ -973,15 +978,17 @@
     lax.fori_loop(0, SLOTS, backward, 0)
     sums = SumAll((r.vec_send, r.vec_recv), 0, r.gvec, r.land_gvec, p)
     sums.begin(0)
-    wqkv_grad(0, r)
-    wqkv_put[0].stage(0)
-    wqkv_grad(1, r)
-    wqkv_put[1].stage(0)
+    for part_of in range(QKV_PARTS):
+        wqkv_grad(part_of, r)
+        wqkv_put[part_of].stage(0)
+        if part_of % 2:
+            act(events.get(("tail", part_of // 2), ()))
     for step in range(1, 4):
         sums.end(step - 1)
         sums.begin(step)
         for piece in wqkv_put:
             piece.stage(step)
+        act(events.get(("tail", step + 1), ()))
     for k in range(1, EXPERTS):
         for piece in put[k]:
             for copy in piece.along_z():
@@ -1054,8 +1061,8 @@
     lax.fori_loop(0, SLOTS, norms, 0)
     wout_grad(r)
     lax.fori_loop(0, SLOTS, backward, 0)
-    for half in range(2):
-        wqkv_grad(half, r)
+    for part in range(QKV_PARTS):
+        wqkv_grad(part, r)
     for name in SHARDS:
         move(getattr(r, name), getattr(r, "out_" + name))
 
@@ -1112,14 +1119,7 @@
     ln1_gain, ln1_bias, w_qkv, b_qv, w_out, b_out, ln2_gain, ln2_bias,
     w_router, w_in, b_in, w_back, b_back,
 ):
-    route_rows = jnp.pad(
-        routes.reshape(SLOTS, SEQ, 2), ((0, 0), (0, ROWS - SEQ), (0, 0)), constant_values=-1
-    ).reshape(TOK, 2)
-    place = priority[0]
-    place = place + (place // SEQ) * (ROWS - SEQ)
-    extra = -place.shape[0] % LANES
-    place_row = jnp.pad(place, (0, extra), constant_values=-1)[None, :]
-    inputs = (image_count, images, cotangent, route_rows, place_row)
+    inputs = (image_count, images, cotangent, routes.T, priority)
     if lax.axis_size("dev") != GROUP:
         return with_collectives(
             inputs, ln1_gain, ln1_bias, w_qkv, b_qv, w_out, b_out, ln2_gain, ln2_bias,

time: 229 us -> 215 us (0.939)
  Pallas kernels: 206 us -> 194 us
    pallas_call x1, Pallas kernels: 206 us -> 194 us  [whole(): pl.pallas_call(whole_kernel, out_shape=[jax.ShapeDtypeStruct(*s) for s in...]
    unnamed x48 -> x59, local copies, waits for them, and re-layouts: 11.6 us -> 12.2 us
where the time goes in v1:
time: 215 us; the launch traced here: 214 us
  Pallas kernels  194 us (90%)
  local copies, waits for them, and re-layouts  17.7 us (8%)
    pallas_call x1, Pallas kernels, whole(): pl.pallas_call(whole_kernel, out_shape=[jax.ShapeDtypeStruct(*s) for s in...  194 us
    unnamed x59, local copies, waits for them, and re-layouts  12.2 us
    reshape x4, local copies, waits for them, and re-layouts, per_device(): v.reshape(s)  5.52 us

profile of v1, /device:TPU:0, one launch (start us, length us, event | category | flops | bytes accessed | tf_op | source)
XLA Modules:
  0.0 214.5 jit_solution(1290323435609614181)
XLA Ops:
  1.4 0.6 copy-done.7
  2.1 1.3 add_bitcast_fusion.refs_5_
  3.4 1.3 reshape.86.refs_7_
  4.7 1.5 reshape.85.refs_6_
  6.2 1.8 reshape.87.refs_8_
  8.1 0.9 reshape.88.refs_9_
  8.9 194.0 %shard_map.289 = (bf16[5,197,512]{2,1,0:T(8,128)(2,1)}, bf16[5,197,512]{2,1,0:T(8,128)(2,1)}, f32[192,128]{1,0:T(8,128)}, f32[64,128]{1,0:T(8,128)}, f32[1024,12...) custom-call(s32[1]{0:T(128)S(6)} %copy.48.refs_0_, ...), custom_call_target="tpu_custom_call" | custom-call | flops 40000000000 | bytes 50000000 | tf_op jit(solution)/shard_map/pallas_call | solution.py:1096
  202.9 2.3 %copy.49 = bf16[5,197,512]{2,1,0:T(8,128)(2,1)} copy(bf16[5,197,512]{2,1,0:T(8,128)(2,1)} %get-tuple-element.60) | data formatting | bytes 2017280
  205.3 1.0 copy.50
  206.2 0.5 copy.51
  206.7 0.2 copy-done.20
  206.9 0.5 copy.52
  207.4 0.6 copy.53
  208.1 0.5 copy.54
  208.6 0.6 copy.55
  209.3 0.5 copy.56
  209.8 0.2 copy-done.17
  209.9 0.5 copy.57
  210.6 0.5 copy.58
  211.2 0.5 copy.59
  211.7 0.8 copy.60
  212.6 0.6 copy.61
  213.1 0.8 copy.62
  214.0 0.5 copy.63
  (41 shorter events, 0.4 us)
Async XLA Ops:
  0.6 0.7 copy-start.10
  0.7 0.7 copy-start.11
  0.7 0.7 copy-start.12
  0.7 0.7 copy-start.13
  1.4 0.7 copy-start.7
  1.4 0.7 copy-start.8
  1.4 0.7 copy-start.9
  6.2 1.8 copy-start.3
  202.9 2.3 %copy-start = (bf16[5,197,512]{2,1,0:T(8,128)(2,1)S(1)}, bf16[5,197,512]{2,1,0:T(8,128)(2,1)}, u32[]{:S(2)}) copy-start(bf16[5,197,512]{2,1,0:T(8,128)(2,1)} %get-tuple-element.61) | copy-start | bytes 3025924
  205.3 1.0 copy-start.21
  205.3 2.2 %copy-start.4 = (f32[192,128]{1,0:T(8,128)S(1)}, f32[192,128]{1,0:T(8,128)}, u32[]{:S(2)}) copy-start(f32[192,128]{1,0:T(8,128)} %get-tuple-element.34) | copy-start | bytes 294916
  205.3 6.5 %copy-start.2 = (f32[1024,128]{1,0:T(8,128)S(1)}, f32[1024,128]{1,0:T(8,128)}, u32[]{:S(2)}) copy-start(f32[1024,128]{1,0:T(8,128)} %get-tuple-element.41) | copy-start | bytes 1572868
  206.2 0.7 copy-start.20
  207.4 0.7 copy-start.19
  207.4 1.2 copy-start.5
  208.6 0.7 copy-start.18
  209.3 0.7 copy-start.17
  209.9 0.6 copy-start.16
  210.6 0.7 copy-start.15
  211.7 0.8 copy-start.6
  211.7 1.4 copy-start.1
  213.1 0.8 copy-start.14

commit v2 on v1

--- a/solution.py
+++ b/solution.py
@@ -1114,6 +1114,57 @@
     )(*inputs, pack, *shards)
 
 
+def arrange_kernel(*refs):
+    lines = refs[-1]
+    for flat, shard in zip(refs[: len(SHARDS)], refs[len(SHARDS) : -1]):
+        rows, columns = shard.shape
+        step = columns // LANES
+        lines[0 : rows * step, :] = flat[...].astype(F32)
+        for j in range(step):
+            shard[:, j * LANES : (j + 1) * LANES] = lines[
+                pl.ds(j, rows, stride=step), :
+            ].astype(BF16)
+
+
+def arrange(flat):
+    vmem = pl.BlockSpec(memory_space=pltpu.VMEM)
+    longest = max(v.shape[0] for v in flat)
+    return pl.pallas_call(
+        arrange_kernel,
+        out_shape=[jax.ShapeDtypeStruct(s, BF16) for s in SHARDS.values()],
+        in_specs=[vmem] * len(flat),
+        out_specs=[vmem] * len(flat),
+        scratch_shapes=[pltpu.VMEM((longest, LANES), F32)],
+    )(*flat)
+
+
+def settle_kernel(*refs):
+    count = (len(refs) - 1) // 3
+    sources, targets, held, sems = refs[:count], refs[count : 2 * count], refs[2 * count : -1], refs[-1]
+    coming = [pltpu.make_async_copy(sources[k], held[k], sems.at[0, k]) for k in range(count)]
+    going = [pltpu.make_async_copy(held[k], targets[k], sems.at[1, k]) for k in range(count)]
+    for copy in coming:
+        copy.start()
+    for arrived, leaving in zip(coming, going):
+        arrived.wait()
+        leaving.start()
+    for copy in going:
+        copy.wait()
+
+
+def settle(arrays):
+    hbm = pl.BlockSpec(memory_space=pltpu.HBM)
+    return pl.pallas_call(
+        settle_kernel,
+        out_shape=[jax.ShapeDtypeStruct(a.shape, a.dtype) for a in arrays],
+        in_specs=[hbm] * len(arrays),
+        out_specs=[hbm] * len(arrays),
+        scratch_shapes=[pltpu.VMEM(a.shape, a.dtype) for a in arrays]
+        + [pltpu.SemaphoreType.DMA((2, len(arrays)))],
+        compiler_params=pltpu.CompilerParams(vmem_limit_bytes=VMEM_LIMIT),
+    )(*arrays)
+
+
 def per_device(
     images, cotangent, routes, priority, image_count,
     ln1_gain, ln1_bias, w_qkv, b_qv, w_out, b_out, ln2_gain, ln2_bias,
@@ -1132,8 +1183,8 @@
         if v is not None:
             pack = pack + jnp.pad(v.astype(F32), (at, 8 * LANES - at - size))
         at += size
-    shards = [v.reshape(s) for v, s in zip((w_qkv, w_out, w_in, w_back), SHARDS.values())]
-    blocks, gimages, *grads = whole(inputs, pack.reshape(8, LANES), shards)
+    shards = arrange([v.reshape(-1, LANES) for v in (w_qkv, w_out, w_in, w_back)])
+    blocks, gimages, *grads = settle(whole(inputs, pack.reshape(8, LANES), shards))
     grads = dict(zip(["w_qkv", "w_out", "w_in", "w_back"] + list(SMALL), grads))
     order = ["ln1_gain", "ln1_bias", "w_qkv", "b_qv", "w_out", "b_out", "ln2_gain", "ln2_bias"]
     order += ["w_router", "w_in", "b_in", "w_back", "b_back"]

time: 215 us -> 203 us (0.944)
  local copies, waits for them, and re-layouts: 17.7 us -> 0.71 us
  Pallas kernels: 194 us -> 199 us
    unnamed x59 -> x18, local copies, waits for them, and re-layouts: 12.2 us -> 0.71 us
    reshape x4 -> x0, local copies, waits for them, and re-layouts: 5.52 us -> none  [per_device(): v.reshape(s)]
    pallas_call x0 -> x2, Pallas kernels: none -> 5.3 us  [the longest x1 3.21 us: settle(): pl.pallas_call(settle_kernel, out_shape=[jax.ShapeDtypeStruct(a.shape, a....]
where the time goes in v2:
time: 203 us; the launch traced here: 202 us
  Pallas kernels  199 us (98%)
    pallas_call x1, Pallas kernels, whole(): pl.pallas_call(whole_kernel, out_shape=[jax.ShapeDtypeStruct(*s) for s in...  194 us

profile of v2, /device:TPU:0, one launch (start us, length us, event | category | flops | bytes accessed | tf_op | source)
XLA Modules:
  0.0 202.3 jit_solution(17006556620561481277)
XLA Ops:
  1.3 0.0 copy-start.7
  1.3 0.0 copy-start.8
  1.3 0.0 copy-start.3
  1.3 0.0 copy-start.4
  1.3 0.0 copy-start.5
  1.3 0.0 copy-start.6
  1.4 0.0 copy-start
  1.4 0.0 copy-start.1
  1.4 0.0 copy-start.2
  1.4 0.6 copy-done.7
  2.0 0.0 copy-done.8
  2.0 0.0 copy-done.3
  2.0 0.0 copy-done.4
  2.0 0.0 copy-done.5
  2.0 0.0 copy-done.6
  2.0 0.0 copy-done
  2.0 0.0 copy-done.1
  2.1 0.0 copy-done.2
  2.1 0.7 add_bitcast_fusion.refs_5_
  2.8 2.1 %shard_map.289 = (bf16[16,1536]{1,0:T(8,128)(2,1)}, bf16[16,512]{1,0:T(8,128)(2,1)}, bf16[64,2048]{1,0:T(8,128)(2,1)}, bf16[256,512]{1,0:T(8,128)(2,1)}) custom-call(bf16[192,128]{1,0:T(8,128)(2,1)} %bitcast.22, bf16[64,128]{1,0:T(8,128)(2,1)} %bitcast.23, bf16[1024,128]{1,0:T(8,128)(2,1)} %bitcast.20, bf16[1024,128]{1,0:T(8,128)(2,1)} %bitcast.21), custom_call_target="tpu_custom_call" | custom-call | tf_op jit(solution)/shard_map/pallas_call | solution.py:1132
  4.8 194.0 %shard_map.290 = (bf16[5,197,512]{2,1,0:T(8,128)(2,1)}, bf16[5,197,512]{2,1,0:T(8,128)(2,1)}, f32[192,128]{1,0:T(8,128)}, f32[64,128]{1,0:T(8,128)}, f32[1024,12...) custom-call(s32[1]{0:T(128)S(6)} %copy.33.refs_0_, ...), custom_call_target="tpu_custom_call" | custom-call | flops 40000000000 | bytes 50000000 | tf_op jit(solution)/shard_map/pallas_call | solution.py:1096
  198.9 3.2 %shard_map.291 = (bf16[5,197,512]{2,1,0:T(8,128)(2,1)}, bf16[5,197,512]{2,1,0:T(8,128)(2,1)}, f32[192,128]{1,0:T(8,128)}, f32[64,128]{1,0:T(8,128)}, f32[1024,12...) custom-call(bf16[5,197,512]{2,1,0:T(8,128)(2,1)} %get-tuple-element., ...), custom_call_target="tpu_custom_call" | custom-call | tf_op jit(solution)/shard_map/pallas_call | solution.py:1157
Async XLA Ops:
  1.3 0.7 copy-start.7
  1.3 0.7 copy-start.8
  1.3 0.7 copy-start.3
  1.3 0.7 copy-start.4
  1.3 0.7 copy-start.5
  1.3 0.7 copy-start.6
  1.4 0.7 copy-start
  1.4 0.7 copy-start.1
  1.4 0.7 copy-start.2

commit v3 on v2

--- a/solution.py
+++ b/solution.py
@@ -442,12 +442,13 @@
     def above(self, k):
         return self.device(self.plane(k), self.y, self.x, self.c)
 
-    def greet(self):
+    def greet(self, meanwhile):
         barrier = pltpu.get_barrier_semaphore()
         friends = [self.above(k) for k in range(1, EXPERTS)]
         friends += [self.core, self.over_y, self.over_x]
         for friend in friends:
             pl.semaphore_signal(barrier, inc=1, device_id=(friend,), device_id_type=MESH)
+        meanwhile()
         pl.semaphore_wait(barrier, len(friends))
 
     def first(self, route):
@@ -753,7 +754,6 @@
     names += ["free_sem", "in_sem", "out_sem"]
     r = Refs(names, refs)
     p = Place()
-    p.greet()
 
     def landing(name):
         return [getattr(r, f"land_{name}_{part}") for part in ("core", "first", "second", "z")]
@@ -818,42 +818,39 @@
         ("expert", 0, 7): [("get", 1, 2, 0)],
         ("combine", 0, 2): [("get", 2, 0, 0), ("get", 1, 2, 1), ("get", 3, -1, 1)],
         ("combine", 0, 3): [("get", 2, 0, 1)],
-        ("combine", 0, 4): [("put", 0, 0, 0)],
+        ("dispatch", 1, 0): [("put", 0, 0, 0)],
         ("dispatch", 1, 4): [("get", 2, 1, 0)],
-        ("expert", 1, 3): [("put", 0, 0, 1)],
+        ("expert", 1, 4): [("put", 0, 0, 1)],
         ("expert", 1, 5): [("get", 3, 0, 1)],
         ("expert", 1, 6): [("get", 2, 2, 0)],
         ("expert", 1, 7): [("get", 2, 1, 1)],
-        ("combine", 1, 0): [("put", 1, 0, 0)],
+        ("combine", 1, 1): [("put", 1, 0, 0)],
         ("combine", 1, 3): [("get", 3, 1, 1)],
-        ("dispatch", 2, 1): [("get", 2, 2, 1), ("put", 0, 1, 0)],
-        ("dispatch", 2, 4): [("put", 1, 0, 1), ("put", 1, 1, 0)],
-        ("expert", 2, 6): [("put", 0, 1, 1)],
-        ("expert", 2, 7): [("get", 3, 2, 1)],
-        ("combine", 2, 2): [("put", 2, 0, 0)],
-        ("combine", 2, 4): [("put", 0, 2, 0)],
-        ("dispatch", 3, 0): [("put", 1, 2, 0)],
-        ("dispatch", 3, 3): [("put", 2, 0, 1)],
-        ("expert", 3, 0): [("put", 2, 1, 0)],
-        ("expert", 3, 3): [("put", 1, 3, 0)],
-        ("expert", 3, 4): [("put", 2, 1, 1)],
-        ("expert", 3, 6): [("put", 0, 3, 0)],
-        ("expert", 3, 7): [("put", 2, 2, 0)],
-        ("combine", 3, 1): [("put", 1, 1, 1)],
-        ("combine", 3, 3): [("put", 3, 0, 0)],
-        ("norms", 0): [("put", 2, 3, 0)],
-        ("norms", 1): [("put", 2, 2, 1)],
-        ("norms", 2): [("put", 3, 1, 0)],
-        ("norms", 3): [("put", 0, 2, 1)],
-        ("backward", 0): [("put", 2, 3, 1)],
-        ("backward", 1): [("put", 3, 0, 1), ("out", 1), ("put", 1, 2, 1)],
-        ("backward", 2): [("put", 3, 2, 0)],
-        ("backward", 3): [("out", 2)],
-        ("backward", 4): [("put", 3, 1, 1), ("put", 1, 3, 1)],
-        ("tail", 0): [("out", 3)],
-        ("tail", 2): [("put", 3, 3, 0)],
-        ("tail", 3): [("put", 3, 2, 1), ("put", 0, 3, 1)],
-        ("tail", 4): [("put", 3, 3, 1)],
+        ("dispatch", 2, 1): [("get", 2, 2, 1)],
+        ("dispatch", 2, 2): [("put", 0, 1, 0)],
+        ("expert", 2, 0): [("put", 1, 0, 1), ("put", 1, 1, 0)],
+        ("expert", 2, 7): [("put", 0, 1, 1), ("get", 3, 2, 1)],
+        ("combine", 2, 3): [("put", 2, 0, 0)],
+        ("dispatch", 3, 0): [("put", 0, 2, 0)],
+        ("dispatch", 3, 1): [("put", 1, 2, 0)],
+        ("dispatch", 3, 4): [("put", 2, 0, 1)],
+        ("expert", 3, 1): [("put", 2, 1, 0)],
+        ("expert", 3, 4): [("put", 1, 3, 0)],
+        ("expert", 3, 5): [("put", 2, 1, 1)],
+        ("expert", 3, 7): [("put", 0, 3, 0)],
+        ("combine", 3, 0): [("put", 2, 2, 0)],
+        ("combine", 3, 2): [("put", 1, 1, 1)],
+        ("combine", 3, 4): [("put", 3, 0, 0)],
+        ("norms", 1): [("put", 2, 3, 0)],
+        ("norms", 2): [("put", 2, 2, 1)],
+        ("norms", 3): [("put", 3, 1, 0)],
+        ("norms", 4): [("put", 0, 2, 1)],
+        ("backward", 1): [("put", 2, 3, 1), ("out", 1)],
+        ("backward", 2): [("put", 3, 0, 1), ("put", 1, 2, 1)],
+        ("backward", 3): [("put", 3, 2, 0), ("out", 2)],
+        ("tail", 0): [("put", 3, 1, 1), ("put", 1, 3, 1), ("out", 3)],
+        ("tail", 3): [("put", 3, 3, 0)],
+        ("tail", 4): [("put", 3, 2, 1), ("put", 0, 3, 1), ("put", 3, 3, 1)],
     }
 
     def beside(*key):
@@ -896,14 +893,18 @@
         copy = piece.local(r.local_sem.at[index])
         copy.start()
         local.append(copy)
+
+    def clear():
+        r.xs[...] = jnp.zeros_like(r.xs)
+        r.gvec[...] = jnp.zeros_like(r.gvec)
+        r.total[...] = jnp.zeros_like(r.total)
+
+    p.greet(clear)
     for piece in flat_get:
         piece.start_z()
     for copy in local:
         copy.wait()
     act(events.get(("start",), ()))
-    r.xs[...] = jnp.zeros_like(r.xs)
-    r.gvec[...] = jnp.zeros_like(r.gvec)
-    r.total[...] = jnp.zeros_like(r.total)
     for step in range(3):
         for piece in flat_get:
             piece.stage(step)

time: 203 us -> 201 us (level)
  no operation moved by 1% of the time
where the time goes in v3:
time: 201 us
  Pallas kernels  198 us (99%)
    pallas_call x1, Pallas kernels, whole(): pl.pallas_call(whole_kernel, out_shape=[jax.ShapeDtypeStruct(*s) for s in...  193 us

profile of v3, /device:TPU:0, one launch (start us, length us, event | category | flops | bytes accessed | tf_op | source)
XLA Modules:
  0.0 201.2 jit_solution(580288445568611046)
XLA Ops:
  1.3 0.0 copy-start.7
  1.3 0.0 copy-start.8
  1.3 0.0 copy-start.3
  1.3 0.0 copy-start.4
  1.3 0.0 copy-start.5
  1.3 0.0 copy-start.6
  1.4 0.0 copy-start
  1.4 0.0 copy-start.1
  1.4 0.0 copy-start.2
  1.4 0.6 copy-done.7
  2.0 0.0 copy-done.8
  2.0 0.0 copy-done.3
  2.0 0.0 copy-done.4
  2.0 0.0 copy-done.5
  2.0 0.0 copy-done.6
  2.0 0.0 copy-done
  2.0 0.0 copy-done.1
  2.1 0.0 copy-done.2
  2.1 0.7 add_bitcast_fusion.refs_5_
  2.8 2.1 %shard_map.289 = (bf16[16,1536]{1,0:T(8,128)(2,1)}, bf16[16,512]{1,0:T(8,128)(2,1)}, bf16[64,2048]{1,0:T(8,128)(2,1)}, bf16[256,512]{1,0:T(8,128)(2,1)}) custom-call(bf16[192,128]{1,0:T(8,128)(2,1)} %bitcast.22, bf16[64,128]{1,0:T(8,128)(2,1)} %bitcast.23, bf16[1024,128]{1,0:T(8,128)(2,1)} %bitcast.20, bf16[1024,128]{1,0:T(8,128)(2,1)} %bitcast.21), custom_call_target="tpu_custom_call" | custom-call | tf_op jit(solution)/shard_map/pallas_call | solution.py:1133
  4.8 192.9 %shard_map.290 = (bf16[5,197,512]{2,1,0:T(8,128)(2,1)}, bf16[5,197,512]{2,1,0:T(8,128)(2,1)}, f32[192,128]{1,0:T(8,128)}, f32[64,128]{1,0:T(8,128)}, f32[1024,12...) custom-call(s32[1]{0:T(128)S(6)} %copy.33.refs_0_, ...), custom_call_target="tpu_custom_call" | custom-call | flops 40000000000 | bytes 50000000 | tf_op jit(solution)/shard_map/pallas_call | solution.py:1097
  197.8 3.2 %shard_map.291 = (bf16[5,197,512]{2,1,0:T(8,128)(2,1)}, bf16[5,197,512]{2,1,0:T(8,128)(2,1)}, f32[192,128]{1,0:T(8,128)}, f32[64,128]{1,0:T(8,128)}, f32[1024,12...) custom-call(bf16[5,197,512]{2,1,0:T(8,128)(2,1)} %get-tuple-element., ...), custom_call_target="tpu_custom_call" | custom-call | tf_op jit(solution)/shard_map/pallas_call | solution.py:1158
Async XLA Ops:
  1.3 0.7 copy-start.7
  1.3 0.7 copy-start.8
  1.3 0.7 copy-start.3
  1.3 0.7 copy-start.4
  1.3 0.7 copy-start.5
  1.3 0.7 copy-start.6
  1.4 0.7 copy-start
  1.4 0.7 copy-start.1
  1.4 0.7 copy-start.2
